TPU v7x, 512 devices: a whole 4x4x16 slice. The times are simulated.
512 devices in a mesh: blk: 256 (over y_lo, x, z, core), rep: 2 (over y_hi).
Axes of the slice: x: 4, y: 4 (y_hi: 2, y_lo: 2; y = y_hi * 2 + y_lo), z: 16, core: 2. Of those that a mesh axis runs over, the one named last changes fastest.
Arguments:
- audio_embed: bfloat16 [2, 65536, 1024], P('rep', 'blk'), may hold values from -0.25 to 0.25
- text_feats: bfloat16 [2, 65536, 768], P('rep', 'blk'), may hold values from -0.25 to 0.25
- text_head: bfloat16 [768, 1024], replicated, may hold values from -0.21875 to 0.21875
- pair_ids: int32 [2, 65536], P('rep', 'blk'), may hold values from 0 to 65535, as said below
- logit_scale: float32 [], replicated, may hold values from 2 to 8
- logit_bias: float32 [], replicated, may hold values from -3 to -1
Outputs:
- grad_audio_embed: bfloat16 [2, 65536, 1024], P('rep', 'blk')
- grad_text_feats: bfloat16 [2, 65536, 768], P('rep', 'blk')
- grad_text_head: bfloat16 [768, 1024], replicated
Inputs may be any that keep to these rules, and one draw needn't show every extreme that they name: `pair_ids`: within every group and block, the pair ids of the block's 256 text rows are the row numbers of that same block's audio rows, each exactly once.
All inputs are finite; a program needn't handle non-finite values.
Results may differ from a plain program's by a relative error of at most 0.015.
Values may be sent and summed in bfloat16 or wider, within the bound.
No kernel may reach another device: no remote copies, remote signals or barrier semaphores. Data moves between devices by JAX's collectives and lax.ppermute only.
A program may use at most 64 MiB of HBM per device.

v0:
```python
import jax
import jax.numpy as jnp
from jax import lax
from jax.sharding import PartitionSpec as P

STEPS = 4


EPS = 1e-06


def from_behind(value, axis, steps):
    count = lax.axis_size(axis)
    pairs = [(source, (source + steps) % count) for source in range(count)]
    return lax.ppermute(value, axis, pairs)


def unit_rows(values):
    wide = values.astype(jnp.float32)
    inverse = lax.rsqrt(jnp.sum(wide * wide, axis=-1, keepdims=True) + EPS)
    return (wide * inverse, inverse)


def pair_weights(audio_blk, text_blk, positive, logit_scale, logit_bias):
    logits = (
        logit_scale
        * lax.dot_general(
            audio_blk, text_blk, (((1,), (1,)), ((), ())), preferred_element_type=jnp.float32
        )
        + logit_bias
    )
    grads = jax.nn.sigmoid(logits) - positive
    return (logit_scale * grads).astype(jnp.bfloat16)


def text_term(weights, audio_blk):
    return lax.dot_general(
        weights, audio_blk, (((0,), (0,)), ((), ())), preferred_element_type=jnp.float32
    )


def body(audio_embed, text_feats, text_head, pair_ids, logit_scale, logit_bias):
    audio = audio_embed[0]
    feats = text_feats[0]
    ident = pair_ids[0]
    rows = audio.shape[0]
    first_row = lax.axis_index("blk") * rows
    audio_unit, audio_inv = unit_rows(audio)
    audio_b = audio_unit.astype(jnp.bfloat16)
    text_proj = jnp.dot(feats, text_head, preferred_element_type=jnp.float32)
    text_unit, text_inv = unit_rows(text_proj)
    text_b = text_unit.astype(jnp.bfloat16)
    owners = first_row + lax.iota(jnp.int32, rows)
    positive = (owners[:, None] == ident[None, :]).astype(jnp.float32)
    nothing = jnp.zeros((rows, rows), jnp.float32)
    audio_grad = jnp.zeros((rows, audio.shape[1]), jnp.float32)
    visiting = text_b
    carried = audio_grad
    for offset in range(STEPS):
        if offset > 0:
            visiting = from_behind(visiting, "blk", 1)
        labels = positive if offset == 0 else nothing
        weights = pair_weights(audio_b, visiting, labels, logit_scale, logit_bias)
        audio_grad = audio_grad + jnp.dot(weights, visiting, preferred_element_type=jnp.float32)
        if offset > 0:
            carried = from_behind(carried, "blk", 1)
        carried = carried + text_term(weights, audio_b)
    text_grad = from_behind(carried.astype(jnp.bfloat16), "blk", 1 - STEPS).astype(carried.dtype)
    grad_audio = (
        (audio_grad - audio_unit * jnp.sum(audio_unit * audio_grad, axis=-1, keepdims=True))
        * audio_inv
    ).astype(jnp.bfloat16)
    proj_grad = (
        (text_grad - text_unit * jnp.sum(text_unit * text_grad, axis=-1, keepdims=True)) * text_inv
    ).astype(jnp.bfloat16)
    grad_feats = lax.dot_general(
        proj_grad, text_head, (((1,), (1,)), ((), ())), preferred_element_type=jnp.float32
    ).astype(jnp.bfloat16)
    head_part = lax.dot_general(
        feats, proj_grad, (((0,), (0,)), ((), ())), preferred_element_type=jnp.float32
    )
    grad_head = lax.psum(head_part, ("blk", "rep")).astype(jnp.bfloat16)
    return (grad_audio[None], grad_feats[None], grad_head)


def solution(mesh):
    return jax.shard_map(
        body,
        mesh=mesh,
        in_specs=(P("rep", "blk", None), P("rep", "blk", None), P(), P("rep", "blk"), P(), P()),
        out_specs=(P("rep", "blk", None), P("rep", "blk", None), P()),
        check_vma=False,
    )
```

profile of v0, /device:TPU:1, one launch (start us, length us, event | category | flops | bytes accessed | tf_op | source)
XLA Modules:
  0.0 292.2 jit_solution(11051697441537613694)
XLA Ops:
  0.6 1.3 fusion.40
  2.2 1.7 multiply_reduce_fusion
  5.4 0.4 fusion.32
  5.8 0.4 fusion.50
  6.2 4.9 %collective-permute-start.3 = (f32[256,1024]{1,0:T(8,128)S(1)}, f32[256,1024]{1,0:T(8,128)S(1)}, u32[]{:S(2)}, u32[]{:S(2)}) collective-permute-start(f32[256,1024]{1,0:T(8,128)S(1)} %fusion.50), channel_id=1, source_target_pairs={{0,2},{2,4},{4,6},{6,8},{8,10},{10,12},{12,14},{14,16},{16,18},{18... | collective-permute-start | bytes 3145736 | tf_op jit(solution)/shard_map/ppermute | solution.py:15
  11.2 1.9 collective-permute-start
  13.1 15.4 %collective-permute-done = bf16[256,1024]{1,0:T(8,128)(2,1)S(1)} collective-permute-done((bf16[256,1024]{1,0:T(8,128)(2,1)S(1)}, bf16[256,1024]{1,0:T(8,128)(2,1)S(1)}, u32[]{:S(2)}, u32[]{:S(2)}) %collective-permute-start) | collective-permute-done | bytes 524320 | tf_op jit(solution)/shard_map/ppermute | solution.py:15
  28.5 0.4 fusion.31
  28.9 0.4 convolution_add_fusion
  29.3 4.4 %collective-permute-start.4 = (f32[256,1024]{1,0:T(8,128)S(1)}, f32[256,1024]{1,0:T(8,128)S(1)}, u32[]{:S(2)}, u32[]{:S(2)}) collective-permute-start(f32[256,1024]{1,0:T(8,128)S(1)} %convolution_add_fusion), channel_id=1, source_target_pairs={{0,2},{2,4},{4,6},{6,8},{8,10},{10,12},{12,14},{14,16},{16,18},{18... | collective-permute-start | bytes 3145736 | tf_op jit(solution)/shard_map/ppermute | solution.py:15
  33.7 1.9 collective-permute-start.1
  35.6 0.3 fusion.56
  35.9 15.1 %collective-permute-done.1 = bf16[256,1024]{1,0:T(8,128)(2,1)S(1)} collective-permute-done((bf16[256,1024]{1,0:T(8,128)(2,1)S(1)}, bf16[256,1024]{1,0:T(8,128)(2,1)S(1)}, u32[]{:S(2)}, u32[]{:S(2)}) %collective-permute-start.1) | collective-permute-done | bytes 524320 | tf_op jit(solution)/shard_map/ppermute | solution.py:15
  51.1 4.4 %collective-permute-start.2 = (bf16[256,1024]{1,0:T(8,128)(2,1)S(1)}, bf16[256,1024]{1,0:T(8,128)(2,1)S(1)}, u32[]{:S(2)}, u32[]{:S(2)}) collective-permute-start(bf16[256,1024]{1,0:T(8,128)(2,1)S(1)} %collective-permute-done.1), channel_id=1, source_target_pairs={{0,2},{2,4},{4,6},{6,8},{8,10},{10,12},{12,14},{14,16},{16,18},{18... | collective-permute-start | bytes 1572872 | tf_op jit(solution)/shard_map/ppermute | solution.py:15
  55.4 0.4 fusion.30
  55.8 0.4 fusion.47
  56.4 1.9 collective-permute-start.5
  58.4 0.3 convolution_add_fusion.3
  58.7 0.3 convolution_add_fusion.2
  59.0 10.9 %collective-permute-done.2 = bf16[256,1024]{1,0:T(8,128)(2,1)S(1)} collective-permute-done((bf16[256,1024]{1,0:T(8,128)(2,1)S(1)}, bf16[256,1024]{1,0:T(8,128)(2,1)S(1)}, u32[]{:S(2)}, u32[]{:S(2)}) %collective-permute-start.2) | collective-permute-done | bytes 524320 | tf_op jit(solution)/shard_map/ppermute | solution.py:15
  69.9 0.4 fusion.29
  70.3 0.4 fusion.45
  70.7 2.9 collective-permute-done.5
  73.8 14.3 %collective-permute-start.6 = (bf16[256,1024]{1,0:T(8,128)(2,1)S(1)}, bf16[256,1024]{1,0:T(8,128)(2,1)S(1)}, u32[]{:S(2)}, u32[]{:S(2)}) collective-permute-start(bf16[256,1024]{1,0:T(8,128)(2,1)S(1)} %add_convert_fusion), channel_id=1, source_target_pairs={{0,506},{2,508},{4,510},{6,0},{8,2},{10,4},{12,6},{14,8},{16,10},{... | collective-permute-start | bytes 1572872 | tf_op jit(solution)/shard_map/ppermute | solution.py:15
  88.1 0.4 fusion.36
  88.5 1.1 fusion.41
  89.6 6.7 %collective-permute-done.6 = bf16[256,1024]{1,0:T(8,128)(2,1)S(1)} collective-permute-done((bf16[256,1024]{1,0:T(8,128)(2,1)S(1)}, bf16[256,1024]{1,0:T(8,128)(2,1)S(1)}, u32[]{:S(2)}, u32[]{:S(2)}) %collective-permute-start.6) | collective-permute-done | bytes 524320 | tf_op jit(solution)/shard_map/ppermute | solution.py:15
  96.3 0.3 fusion.33
  96.9 1.4 fusion.3
  98.2 2.3 convolution_bitcast_fusion
  100.5 190.1 %all-reduce.1 = bf16[768,1024]{0,1:T(8,128)(2,1)S(1)} all-reduce(f32[768,1024]{0,1:T(8,128)} %convolution_bitcast_fusion), channel_id=1, replica_groups=mesh['blk'=256,'rep'=2] {'blk','rep'}, use_global_device_ids=true, to_apply=%region_4.0 | all-reduce | flops 786432 | bytes 4718592 | tf_op jit(solution)/shard_map/psum | solution.py:82
  290.6 1.6 copy.9
  (17 shorter events, 1.0 us)
Async XLA Ops:
  0.6 1.6 copy-start
  2.2 3.2 %copy-start.1 = (bf16[1,256,1024]{2,1,0:T(8,128)(2,1)S(1)}, bf16[1,256,1024]{2,1,0:T(8,128)(2,1)}, u32[]{:S(2)}) copy-start(bf16[1,256,1024]{2,1,0:T(8,128)(2,1)} %param.6) | copy-start | bytes 1572868
  2.2 3.2 %copy-start.3 = (s32[1,256]{1,0:T(1,128)S(1)}, s32[1,256]{1,0:T(1,128)}, u32[]{:S(2)}) copy-start(s32[1,256]{1,0:T(1,128)} %param.9) | copy-start | bytes 3076
  6.2 22.7 %collective-permute-start.3 = (f32[256,1024]{1,0:T(8,128)S(1)}, f32[256,1024]{1,0:T(8,128)S(1)}, u32[]{:S(2)}, u32[]{:S(2)}) collective-permute-start(f32[256,1024]{1,0:T(8,128)S(1)} %fusion.50), channel_id=1, source_target_pairs={{0,2},{2,4},{4,6},{6,8},{8,10},{10,12},{12,14},{14,16},{16,18},{18... | collective-permute-start | bytes 3145736 | tf_op jit(solution)/shard_map/ppermute | solution.py:15
  11.2 17.3 %collective-permute-start = (bf16[256,1024]{1,0:T(8,128)(2,1)S(1)}, bf16[256,1024]{1,0:T(8,128)(2,1)S(1)}, u32[]{:S(2)}, u32[]{:S(2)}) collective-permute-start(bf16[256,1024]{1,0:T(8,128)(2,1)S(1)} %multiply_convert_fusion), channel_id=1, source_target_pairs={{0,2},{2,4},{4,6},{6,8},{8,10},{10,12},{12,14},{14,16},{16,18},{18... | collective-permute-start | bytes 1572872 | tf_op jit(solution)/shard_map/ppermute | solution.py:15
  29.3 26.9 %collective-permute-start.4 = (f32[256,1024]{1,0:T(8,128)S(1)}, f32[256,1024]{1,0:T(8,128)S(1)}, u32[]{:S(2)}, u32[]{:S(2)}) collective-permute-start(f32[256,1024]{1,0:T(8,128)S(1)} %convolution_add_fusion), channel_id=1, source_target_pairs={{0,2},{2,4},{4,6},{6,8},{8,10},{10,12},{12,14},{14,16},{16,18},{18... | collective-permute-start | bytes 3145736 | tf_op jit(solution)/shard_map/ppermute | solution.py:15
  33.7 17.3 %collective-permute-start.1 = (bf16[256,1024]{1,0:T(8,128)(2,1)S(1)}, bf16[256,1024]{1,0:T(8,128)(2,1)S(1)}, u32[]{:S(2)}, u32[]{:S(2)}) collective-permute-start(bf16[256,1024]{1,0:T(8,128)(2,1)S(1)} %collective-permute-done), channel_id=1, source_target_pairs={{0,2},{2,4},{4,6},{6,8},{8,10},{10,12},{12,14},{14,16},{16,18},{18... | collective-permute-start | bytes 1572872 | tf_op jit(solution)/shard_map/ppermute | solution.py:15
  51.1 18.9 %collective-permute-start.2 = (bf16[256,1024]{1,0:T(8,128)(2,1)S(1)}, bf16[256,1024]{1,0:T(8,128)(2,1)S(1)}, u32[]{:S(2)}, u32[]{:S(2)}) collective-permute-start(bf16[256,1024]{1,0:T(8,128)(2,1)S(1)} %collective-permute-done.1), channel_id=1, source_target_pairs={{0,2},{2,4},{4,6},{6,8},{8,10},{10,12},{12,14},{14,16},{16,18},{18... | collective-permute-start | bytes 1572872 | tf_op jit(solution)/shard_map/ppermute | solution.py:15
  56.4 17.2 %collective-permute-start.5 = (f32[256,1024]{1,0:T(8,128)S(1)}, f32[256,1024]{1,0:T(8,128)S(1)}, u32[]{:S(2)}, u32[]{:S(2)}) collective-permute-start(f32[256,1024]{1,0:T(8,128)S(1)} %add.93), channel_id=1, source_target_pairs={{0,2},{2,4},{4,6},{6,8},{8,10},{10,12},{12,14},{14,16},{16,18},{18... | collective-permute-start | bytes 3145736 | tf_op jit(solution)/shard_map/ppermute | solution.py:15
  73.8 22.5 %collective-permute-start.6 = (bf16[256,1024]{1,0:T(8,128)(2,1)S(1)}, bf16[256,1024]{1,0:T(8,128)(2,1)S(1)}, u32[]{:S(2)}, u32[]{:S(2)}) collective-permute-start(bf16[256,1024]{1,0:T(8,128)(2,1)S(1)} %add_convert_fusion), channel_id=1, source_target_pairs={{0,506},{2,508},{4,510},{6,0},{8,2},{10,4},{12,6},{14,8},{16,10},{... | collective-permute-start | bytes 1572872 | tf_op jit(solution)/shard_map/ppermute | solution.py:15
  96.9 1.4 copy-start.2
where the time goes:
time: 293 us; the launch traced here: 292 us
  blocking collectives  190 us (65%)
  waiting for transfers between devices  51 us (17%)
  starting transfers between devices  33.8 us (12%)
  matrix products  9.86 us (3%)
  other arithmetic  3.42 us (1%)
    psum x1, blocking collectives, body(): grad_head = lax.psum(head_part, ('blk', 'rep')).astype(jnp.bfloat16)  190 us
    ppermute x7, waiting for transfers between devices, from_behind(): return lax.ppermute(value, axis, pairs)  51 us
    ppermute x7, starting transfers between devices, from_behind(): return lax.ppermute(value, axis, pairs)  33.8 us
  transfers between devices with their start and end apart: 7, of which 5 were waited for; matrix products, arithmetic and copies ran while one was open for 2% of the time, Pallas kernels for 0%

commit v1 on v0

v1 whole, which is shorter than its diff:
```python
import jax
import jax.numpy as jnp
from jax import lax
from jax.sharding import Mesh, PartitionSpec as P

EPS = 1e-06
BLK = ("yl", "x", "z", "c")
PLANE = ("yl", "x", "yh")


def shifted(value, steps):
    count = lax.axis_size(BLK)
    return lax.ppermute(value, BLK, [(i, (i + steps) % count) for i in range(count)])


def other_core(value):
    return lax.ppermute(value, "c", [(0, 1), (1, 0)])


def even_odd(value, even, odd):
    count = lax.axis_size(BLK)
    return lax.ppermute(
        value, BLK, [(i, (i + (odd if i % 2 else even)) % count) for i in range(count)]
    )


def unit_rows(values):
    wide = values.astype(jnp.float32)
    inverse = lax.rsqrt(jnp.sum(wide * wide, axis=-1, keepdims=True) + EPS)
    return (wide * inverse, inverse)


def dot(a, b, da, db):
    return lax.dot_general(a, b, (((da,), (db,)), ((), ())), preferred_element_type=jnp.float32)


def pair_weights(audio_blk, text_blk, positive, scale, bias):
    grads = jax.nn.sigmoid(scale * dot(audio_blk, text_blk, 1, 1) + bias)
    if positive is not None:
        grads = grads - positive
    return (scale * grads).astype(jnp.bfloat16)


def body(audio_embed, text_feats, text_head, pair_ids, scale, bias):
    audio = audio_embed[0]
    feats = text_feats[0]
    ident = pair_ids[0]
    rows = audio.shape[0]
    core = lax.axis_index("c")
    first_row = lax.axis_index(BLK) * rows

    text_2 = shifted(feats, 2)
    audio_2 = shifted(audio, -2)
    text_a = even_odd(feats, 1, 3)
    audio_a = even_odd(audio, -3, -1)
    text_b = other_core(text_2)
    audio_b = other_core(audio_2)

    def project(block):
        unit, inv = unit_rows(jnp.dot(block, text_head, preferred_element_type=jnp.float32))
        return unit, inv, unit.astype(jnp.bfloat16)

    def audio_rows(block):
        return unit_rows(block)[0].astype(jnp.bfloat16)

    audio_unit, audio_inv = unit_rows(audio)
    own_audio = audio_unit.astype(jnp.bfloat16)
    text_unit, text_inv, own_text = project(feats)
    owners = first_row + lax.iota(jnp.int32, rows)
    positive = (owners[:, None] == ident[None, :]).astype(jnp.float32)
    weights = pair_weights(own_audio, own_text, positive, scale, bias)
    audio_grad = dot(weights, own_text, 1, 0)
    text_grad = dot(weights, own_audio, 0, 0)
    for block in (text_2, text_a, text_b):
        other = project(block)[2]
        audio_grad += dot(pair_weights(own_audio, other, None, scale, bias), other, 1, 0)
    for block in (audio_2, audio_a, audio_b):
        other = audio_rows(block)
        text_grad += dot(pair_weights(other, own_text, None, scale, bias), other, 0, 0)
    grad_audio = (
        (audio_grad - audio_unit * jnp.sum(audio_unit * audio_grad, axis=-1, keepdims=True))
        * audio_inv
    ).astype(jnp.bfloat16)
    proj_grad = (
        (text_grad - text_unit * jnp.sum(text_unit * text_grad, axis=-1, keepdims=True)) * text_inv
    ).astype(jnp.bfloat16)
    grad_feats = dot(proj_grad, text_head, 1, 1).astype(jnp.bfloat16)

    wide = proj_grad.shape[1]
    half = wide // 2
    mine = lax.dynamic_slice_in_dim(proj_grad, core * half, half, 1)
    theirs = lax.dynamic_slice_in_dim(proj_grad, (1 - core) * half, half, 1)
    sent = other_core(dot(feats, theirs, 0, 0).astype(jnp.bfloat16))
    part = (dot(feats, mine, 0, 0) + sent.astype(jnp.float32)).astype(jnp.bfloat16)
    plane = lax.axis_size(PLANE)
    depth = part.shape[0] // plane
    tiles = lax.all_to_all(part.reshape(plane, depth, half), PLANE, 0, 0, tiled=True)
    tile = jnp.sum(tiles.astype(jnp.float32), axis=0).astype(jnp.bfloat16)
    line = lax.all_gather(tile, "z", axis=0)
    total = jnp.sum(line.astype(jnp.float32), axis=0).astype(jnp.bfloat16)
    spread = lax.all_to_all(
        jnp.broadcast_to(total, (plane, depth, half)), PLANE, 0, 0, tiled=True
    ).reshape(plane * depth, half)
    other_half = other_core(spread)
    left = jnp.where(core == 0, spread, other_half)
    right = jnp.where(core == 0, other_half, spread)
    grad_head = jnp.concatenate([left, right], axis=1)
    return (grad_audio[None], grad_feats[None], grad_head)


def solution(mesh):
    fine = Mesh(mesh.devices.reshape(2, 4, 16, 2, 2), ("yl", "x", "z", "c", "yh"))
    rows = P("yh", BLK, None)
    return jax.shard_map(
        body,
        mesh=fine,
        in_specs=(rows, rows, P(), P("yh", BLK), P(), P()),
        out_specs=(rows, rows, P()),
        check_vma=False,
    )
```

time: 293 us -> 164 us (0.56)
  blocking collectives: 190 us -> 30.4 us
  waiting for transfers between devices: 51 us -> 15.4 us
  matrix products: 9.86 us -> 37.5 us
  starting transfers between devices: 33.8 us -> 57.7 us
  other arithmetic: 3.42 us -> 15.1 us
  local copies, waits for them, and re-layouts: 1.85 us -> 4.81 us
    psum x1 -> x0, blocking collectives: 190 us -> none  [body(): grad_head = lax.psum(head_part, ('blk', 'rep')).astype(jnp.bfloat16)]
    ppermute x7 -> x8, waiting for transfers between devices: 51 us -> 0.02 us  [the longest x4 0.01 us: other_core(): return lax.ppermute(value, 'c', [(0, 1), (1, 0)])]
    all_gather x0 -> x1, blocking collectives: none -> 30.4 us  [body(): line = lax.all_gather(tile, 'z', axis=0)]
    dot_general x15 -> x16, matrix products: 9.86 us -> 37.5 us  [the longest x12 29.9 us: dot(): lax.dot_general(a, b, (((da,), (db,)), ((), ())), preferred_element_type=...]
    all_to_all x0 -> x2, waiting for transfers between devices: none -> 15.4 us  [the longest x1 9.72 us: body(): lax.all_to_all(part.reshape(plane, depth, half), PLANE, 0, 0, tiled=True)]
    ppermute x7 -> x8, starting transfers between devices: 33.8 us -> 48.3 us  [the longest x4 26.3 us: other_core(): return lax.ppermute(value, 'c', [(0, 1), (1, 0)])]
    all_to_all x0 -> x2, starting transfers between devices: none -> 9.4 us  [the longest x1 5.11 us: body(): lax.all_to_all(jnp.broadcast_to(total, (plane, depth, half)), PLANE, 0, 0...]
    reduce_sum x1 -> x4, other arithmetic: 1.34 us -> 4.9 us  [unit_rows(): inverse = lax.rsqrt(jnp.sum(wide * wide, axis=-1, keepdims=True) + EPS)]
  transfers between devices with their start and end apart: 7 -> 10, of which waited for: 5 -> 2; matrix products, arithmetic and copies ran while one was open for 2% -> 33% of each run, Pallas kernels for 0% -> 0%
where the time goes in v1:
time: 164 us; the launch traced here: 163 us
  starting transfers between devices  57.7 us (35%)
  matrix products  37.5 us (23%)
  blocking collectives  30.4 us (19%)
  waiting for transfers between devices  15.4 us (9%)
  other arithmetic  15.1 us (9%)
  local copies, waits for them, and re-layouts  4.81 us (3%)
  between operations  2.19 us (1%)
    all_gather x1, blocking collectives, body(): line = lax.all_gather(tile, 'z', axis=0)  30.4 us
    dot_general x12, matrix products, dot(): lax.dot_general(a, b, (((da,), (db,)), ((), ())), preferred_element_type=...  29.9 us
    ppermute x4, starting transfers between devices, other_core(): return lax.ppermute(value, 'c', [(0, 1), (1, 0)])  26.3 us
    ppermute x2, starting transfers between devices, shifted(): lax.ppermute(value, BLK, [(i, (i + steps) % count) for i in range(count)])  13.4 us
    all_to_all x1, waiting for transfers between devices, body(): lax.all_to_all(part.reshape(plane, depth, half), PLANE, 0, 0, tiled=True)  9.72 us
    ppermute x2, starting transfers between devices, even_odd(): lax.ppermute(value, BLK, [(i, (i + (odd if i % 2 else even)) % count) for...  8.61 us
    dot_general x4, matrix products, project(): jnp.dot(block, text_head, preferred_element_type=jnp.float32)  7.63 us
    all_to_all x1, waiting for transfers between devices, body(): lax.all_to_all(jnp.broadcast_to(total, (plane, depth, half)), PLANE, 0, 0...  5.67 us
  transfers between devices with their start and end apart: 10, of which 2 were waited for; matrix products, arithmetic and copies ran while one was open for 33% of the time, Pallas kernels for 0%

profile of v1, /device:TPU:1, one launch (start us, length us, event | category | flops | bytes accessed | tf_op | source)
XLA Modules:
  0.0 163.1 jit_solution(2969430743249717458)
XLA Ops:
  0.6 4.5 %collective-permute-start = (bf16[256,768]{1,0:T(8,128)(2,1)}, bf16[256,768]{1,0:T(8,128)(2,1)}, u32[]{:S(2)}, u32[]{:S(2)}) collective-permute-start(bf16[256,768]{1,0:T(8,128)(2,1)} %bitcast.58), channel_id=1, source_target_pairs={{0,4},{2,6},{4,8},{6,10},{8,12},{10,14},{12,16},{14,18},{16,20},{1... | collective-permute-start | bytes 1179656 | tf_op jit(solution)/shard_map/ppermute | solution.py:13
  5.2 5.7 %collective-permute-start.1 = (bf16[256,768]{1,0:T(8,128)(2,1)}, bf16[256,768]{1,0:T(8,128)(2,1)}, u32[]{:S(2)}, u32[]{:S(2)}) collective-permute-start(bf16[256,768]{1,0:T(8,128)(2,1)} %bitcast.59), channel_id=1, source_target_pairs={{0,2},{2,8},{4,6},{6,12},{8,10},{10,16},{12,14},{14,20},{16,18},{1... | collective-permute-start | bytes 1179656 | tf_op jit(solution)/shard_map/ppermute | solution.py:22
  10.9 8.9 %collective-permute-start.3 = (bf16[256,1024]{1,0:T(8,128)(2,1)}, bf16[256,1024]{1,0:T(8,128)(2,1)}, u32[]{:S(2)}, u32[]{:S(2)}) collective-permute-start(bf16[256,1024]{1,0:T(8,128)(2,1)} %bitcast.56), channel_id=1, source_target_pairs={{0,508},{2,510},{4,0},{6,2},{8,4},{10,6},{12,8},{14,10},{16,12},{1... | collective-permute-start | bytes 1572872 | tf_op jit(solution)/shard_map/ppermute | solution.py:13
  19.8 2.9 %collective-permute-start.4 = (bf16[256,1024]{1,0:T(8,128)(2,1)}, bf16[256,1024]{1,0:T(8,128)(2,1)}, u32[]{:S(2)}, u32[]{:S(2)}) collective-permute-start(bf16[256,1024]{1,0:T(8,128)(2,1)} %bitcast.57), channel_id=1, source_target_pairs={{0,506},{2,0},{4,510},{6,4},{8,2},{10,8},{12,6},{14,12},{16,10},{1... | collective-permute-start | bytes 1572872 | tf_op jit(solution)/shard_map/ppermute | solution.py:22
  24.0 1.7 %multiply_reduce_fusion.4 = (f32[256]{0:T(256)S(1)}, f32[256,1024]{1,0:T(8,128)S(1)}) fusion(bf16[768,1024]{1,0:T(8,128)(2,1)S(1)} %copy-done, bf16[1,256,768]{2,1,0:T(8,128)(2,1)} %param.7), kind=kOutput, calls=%fused_computation.100 | convolution fusion | flops 403177216 | bytes 3015680 | tf_op jit(solution)/shard_map/dot_general | solution.py:60
  27.9 1.5 fusion.55
  30.1 1.4 fusion.118
  31.4 5.6 %collective-permute-start.5 = (bf16[256,1024]{1,0:T(8,128)(2,1)}, bf16[256,1024]{1,0:T(8,128)(2,1)}, u32[]{:S(2)}, u32[]{:S(2)}) collective-permute-start(bf16[256,1024]{1,0:T(8,128)(2,1)} %collective-permute-done.3), channel_id=1, source_target_pairs={{0,2},{2,0},{1,3},{3,1},{4,6},{6,4},{5,7},{7,5},{8,10},{10,8},{9,1... | collective-permute-start | bytes 1572872 | tf_op jit(solution)/shard_map/ppermute | solution.py:17
  39.5 3.7 %convolution_add_fusion.2 = f32[256,1024]{1,0:T(8,128)} fusion(f32[256,1024]{1,0:T(8,128)} %fusion.118, bf16[256,1024]{1,0:T(8,128)(2,1)} %multiply_convert_fusion.4, bf16[256,1024]{1,0:T(8,128)(2,1)} %collective-permute-done.3, f32[256]{0:T(256)S(1)} %add_rsqrt_fusion.2, f32[]{:T(128)S(6)} %copy.12, f32[]{:T(128)S(6)} %copy.11), kind=kOutput, calls=%fused_computation.6 | convolution fusion | flops 270729216 | bytes 3146760 | tf_op jit(solution)/shard_map/dot_general | solution.py:34
  43.1 3.6 %convolution_add_fusion.1 = f32[256,1024]{1,0:T(8,128)} fusion(f32[256,1024]{1,0:T(8,128)} %convolution_add_fusion.2, bf16[256,1024]{1,0:T(8,128)(2,1)} %multiply_convert_fusion.4, bf16[256,1024]{1,0:T(8,128)(2,1)} %collective-permute-done.4, f32[256]{0:T(256)S(1)} %add_rsqrt_fusion.1, f32[]{:T(128)S(6)} %copy.12, f32[]{:T(128)S(6)} %copy.11), kind=kOutput, calls=%fused_computation.5 | convolution fusion | flops 270729216 | bytes 3146760 | tf_op jit(solution)/shard_map/dot_general | solution.py:34
  47.9 3.6 %multiply_reduce_fusion = (f32[256]{0:T(256)S(1)}, f32[256,1024]{1,0:T(8,128)}) fusion(f32[256,1024]{1,0:T(8,128)S(1)} %get-tuple-element.6, f32[256]{0:T(256)S(1)} %add_rsqrt_fusion.6, f32[256,1024]{1,0:T(8,128)} %convolution_add_fusion.1, bf16[256,1024]{1,0:T(8,128)(2,1)} %collective-permute-done.5, f32[256]{0:T(256)S(1)} %add_rsqrt_fusion, ...), kind=kOutput, calls=%fused_computation.93 | convolution fusion | flops 271515392 | bytes 4197384 | tf_op jit(solution)/shard_map/dot_general | solution.py:34
  51.5 1.5 multiply_convert_fusion
  55.2 7.1 %collective-permute-start.6 = (bf16[768,512]{0,1:T(8,128)(2,1)}, bf16[768,512]{0,1:T(8,128)(2,1)}, u32[]{:S(2)}, u32[]{:S(2)}) collective-permute-start(bf16[768,512]{0,1:T(8,128)(2,1)} %fusion.4), channel_id=1, source_target_pairs={{0,2},{2,0},{1,3},{3,1},{4,6},{6,4},{5,7},{7,5},{8,10},{10,8},{9,1... | collective-permute-start | bytes 2359304 | tf_op jit(solution)/shard_map/ppermute | solution.py:17
  63.6 1.9 %collective-permute-start.2 = (bf16[256,768]{1,0:T(8,128)(2,1)}, bf16[256,768]{1,0:T(8,128)(2,1)}, u32[]{:S(2)}, u32[]{:S(2)}) collective-permute-start(bf16[256,768]{1,0:T(8,128)(2,1)} %collective-permute-done), channel_id=1, source_target_pairs={{0,2},{2,0},{1,3},{3,1},{4,6},{6,4},{5,7},{7,5},{8,10},{10,8},{9,1... | collective-permute-start | bytes 1179656 | tf_op jit(solution)/shard_map/ppermute | solution.py:17
  65.6 2.6 %multiply_reduce_fusion.3 = (f32[256]{0:T(256)S(1)}, f32[256,1024]{1,0:T(8,128)}) fusion(bf16[256,768]{1,0:T(8,128)(2,1)} %collective-permute-done, bf16[768,1024]{1,0:T(8,128)(2,1)S(1)} %copy-done), kind=kOutput, calls=%fused_computation.99 | convolution fusion | flops 403177216 | bytes 3015680 | tf_op jit(solution)/shard_map/dot_general | solution.py:60
  68.1 1.7 %multiply_reduce_fusion.2 = (f32[256]{0:T(256)S(1)}, f32[256,1024]{1,0:T(8,128)S(1)}) fusion(bf16[256,768]{1,0:T(8,128)(2,1)} %collective-permute-done.1, bf16[768,1024]{1,0:T(8,128)(2,1)S(1)} %copy-done), kind=kOutput, calls=%fused_computation.97 | convolution fusion | flops 403177216 | bytes 3015680 | tf_op jit(solution)/shard_map/dot_general | solution.py:60
  69.9 2.4 %fusion = bf16[768,512]{0,1:T(8,128)(2,1)} fusion(bf16[768,512]{0,1:T(8,128)(2,1)} %collective-permute-done.6, bf16[256,1024]{1,0:T(8,128)(2,1)S(1)} %copy-done.5, s32[]{:T(128)S(6)} %select_n.19, bf16[1,256,768]{2,1,0:T(8,128)(2,1)S(1)} %copy-done.3), kind=kOutput, calls=%fused_computation.2 | convolution fusion | flops 202506240 | bytes 2228228 | tf_op jit(solution)/shard_map/dot_general | solution.py:34
  72.3 2.3 %copy.10 = bf16[768,512]{1,0:T(8,128)(2,1)} copy(bf16[768,512]{0,1:T(8,128)(2,1)} %fusion) | data formatting | bytes 1572864 | tf_op jit(solution)/shard_map/convert_element_type | solution.py:94
  74.6 4.3 %all-to-all-start = ((bf16[16,48,512]{2,1,0:T(8,128)(2,1)}), bf16[16,48,512]{2,1,0:T(8,128)(2,1)}, u32[]{:S(2)}, u32[]{:S(2)}) async-start(bf16[16,48,512]{2,1,0:T(8,128)(2,1)} %bitcast.60), calls=%async_computation | async-start | bytes 1572864 | tf_op jit(solution)/shard_map/all_to_all | solution.py:97
  79.0 3.7 %convolution_add_fusion.5 = f32[256,1024]{1,0:T(8,128)} fusion(f32[256,1024]{1,0:T(8,128)} %fusion.131, f32[256,1024]{1,0:T(8,128)} %get-tuple-element.8, f32[256]{0:T(256)S(1)} %add_rsqrt_fusion.5, f32[]{:T(128)S(6)} %copy.12, f32[]{:T(128)S(6)} %copy.11, f32[256]{0:T(256)S(1)} %add_rsqrt_fusion.7, bf16[1,256,1024]{2,1,0:T(8,128)(2,1)S(1)} %copy-done.1), kind=kOutput, calls=%fused_computation.9 | convolution fusion | flops 270991360 | bytes 3672072 | tf_op jit(solution)/shard_map/dot_general | solution.py:34
  82.7 9.7 %all-to-all-done = bf16[16,48,512]{2,1,0:T(8,128)(2,1)} async-done(((bf16[16,48,512]{2,1,0:T(8,128)(2,1)}), bf16[16,48,512]{2,1,0:T(8,128)(2,1)}, u32[]{:S(2)}, u32[]{:S(2)}) %all-to-all-start) | async-done | bytes 786464 | tf_op jit(solution)/shard_map/all_to_all | solution.py:97
  93.6 30.4 %all-gather = bf16[768,512]{1,0:T(8,128)(2,1)} all-gather(bf16[48,512]{1,0:T(8,128)(2,1)S(1)} %reduce_sum.124), channel_id=2, replica_groups=mesh['yl'=2,'x'=4,'z'=16,'c'=2,'yh'=2] {'z'}, dimensions={0}, use_global_device_ids=true | all-gather | bytes 835584 | tf_op jit(solution)/shard_map/all_gather | solution.py:99
  126.2 5.1 %all-to-all-start.1 = ((bf16[16,48,512]{2,1,0:T(8,128)(2,1)}), bf16[16,48,512]{2,1,0:T(8,128)(2,1)}, u32[]{:S(2)}, u32[]{:S(2)}) async-start(bf16[16,48,512]{2,1,0:T(8,128)(2,1)} %broadcast_in_dim.8), calls=%async_computation.1 | async-start | bytes 1572864 | tf_op jit(solution)/shard_map/all_to_all | solution.py:101
  131.3 3.1 %convolution_add_fusion.4 = f32[256,1024]{1,0:T(8,128)} fusion(f32[256,1024]{1,0:T(8,128)} %convolution_add_fusion.5, f32[256,1024]{1,0:T(8,128)S(1)} %get-tuple-element.10, f32[256]{0:T(256)S(1)} %add_rsqrt_fusion.4, f32[]{:T(128)S(6)} %copy.12, f32[]{:T(128)S(6)} %copy.11, f32[256]{0:T(256)S(1)} %add_rsqrt_fusion.7, bf16[1,256,1024]{2,1,0:T(8,128)(2,1)S(1)} %copy-done.1), kind=kOutput, calls=%fused_computation.8 | convolution fusion | flops 270991360 | bytes 3672072 | tf_op jit(solution)/shard_map/dot_general | solution.py:34
  134.4 1.7 %multiply_reduce_fusion.1 = (f32[256]{0:T(256)S(1)}, f32[256,1024]{1,0:T(8,128)S(1)}) fusion(bf16[256,768]{1,0:T(8,128)(2,1)} %collective-permute-done.2, bf16[768,1024]{1,0:T(8,128)(2,1)S(1)} %copy-done), kind=kOutput, calls=%fused_computation.95 | convolution fusion | flops 403177216 | bytes 3015680 | tf_op jit(solution)/shard_map/dot_general | solution.py:60
  136.1 5.7 %all-to-all-done.1 = bf16[16,48,512]{2,1,0:T(8,128)(2,1)} async-done(((bf16[16,48,512]{2,1,0:T(8,128)(2,1)}), bf16[16,48,512]{2,1,0:T(8,128)(2,1)}, u32[]{:S(2)}, u32[]{:S(2)}) %all-to-all-start.1) | async-done | bytes 786464 | tf_op jit(solution)/shard_map/all_to_all | solution.py:101
  141.8 11.7 %collective-permute-start.7 = (bf16[768,512]{1,0:T(8,128)(2,1)}, bf16[768,512]{1,0:T(8,128)(2,1)}, u32[]{:S(2)}, u32[]{:S(2)}) collective-permute-start(bf16[768,512]{1,0:T(8,128)(2,1)} %bitcast.9), channel_id=1, source_target_pairs={{0,2},{2,0},{1,3},{3,1},{4,6},{6,4},{5,7},{7,5},{8,10},{10,8},{9,1... | collective-permute-start | bytes 2359304 | tf_op jit(solution)/shard_map/ppermute | solution.py:17
  153.5 3.1 %fusion.56 = (f32[256]{0:T(256)S(1)}, f32[256,1024]{1,0:T(8,128)}) fusion(f32[256]{0:T(256)S(1)} %add_rsqrt_fusion.7, bf16[1,256,1024]{2,1,0:T(8,128)(2,1)S(1)} %copy-done.1, f32[256,1024]{1,0:T(8,128)} %convolution_add_fusion.4, f32[256,1024]{1,0:T(8,128)S(1)} %get-tuple-element.12, f32[256]{0:T(256)S(1)} %add_rsqrt_fusion.3, f32[]{:T(128)S(6)} %copy.12, ...), kind=kOutput, calls=%fused_computation.81 | convolution fusion | flops 272039680 | bytes 3673096 | tf_op jit(solution)/shard_map/dot_general | solution.py:34
  156.6 2.3 %fusion.73 = bf16[1,256,1024]{2,1,0:T(8,128)(2,1)} fusion(f32[256,1024]{1,0:T(8,128)} %get-tuple-element.14, f32[256]{0:T(256)S(1)} %get-tuple-element.13, f32[256]{0:T(256)S(1)} %add_rsqrt_fusion.7, bf16[1,256,1024]{2,1,0:T(8,128)(2,1)S(1)} %copy-done.1), kind=kLoop, calls=%fused_computation.104 | loop fusion | flops 1572864 | bytes 2099200 | tf_op jit(solution)/shard_map/broadcast_in_dim | solution.py:108
  158.9 1.4 fusion.5
  160.3 1.5 broadcast_select_fusion.1
  161.8 1.4 pad_maximum_fusion
  (47 shorter events, 13.4 us)
Async XLA Ops:
  0.6 23.3 %copy-start = (bf16[768,1024]{1,0:T(8,128)(2,1)S(1)}, bf16[768,1024]{1,0:T(8,128)(2,1)}, u32[]{:S(2)}) copy-start(bf16[768,1024]{1,0:T(8,128)(2,1)} %param.8) | copy-start | bytes 4718596
  0.6 63.0 %collective-permute-start = (bf16[256,768]{1,0:T(8,128)(2,1)}, bf16[256,768]{1,0:T(8,128)(2,1)}, u32[]{:S(2)}, u32[]{:S(2)}) collective-permute-start(bf16[256,768]{1,0:T(8,128)(2,1)} %bitcast.58), channel_id=1, source_target_pairs={{0,4},{2,6},{4,8},{6,10},{8,12},{10,14},{12,16},{14,18},{16,20},{1... | collective-permute-start | bytes 1179656 | tf_op jit(solution)/shard_map/ppermute | solution.py:13
  5.2 63.0 %collective-permute-start.1 = (bf16[256,768]{1,0:T(8,128)(2,1)}, bf16[256,768]{1,0:T(8,128)(2,1)}, u32[]{:S(2)}, u32[]{:S(2)}) collective-permute-start(bf16[256,768]{1,0:T(8,128)(2,1)} %bitcast.59), channel_id=1, source_target_pairs={{0,2},{2,8},{4,6},{6,12},{8,10},{10,16},{12,14},{14,20},{16,18},{1... | collective-permute-start | bytes 1179656 | tf_op jit(solution)/shard_map/ppermute | solution.py:22
  10.9 20.5 %collective-permute-start.3 = (bf16[256,1024]{1,0:T(8,128)(2,1)}, bf16[256,1024]{1,0:T(8,128)(2,1)}, u32[]{:S(2)}, u32[]{:S(2)}) collective-permute-start(bf16[256,1024]{1,0:T(8,128)(2,1)} %bitcast.56), channel_id=1, source_target_pairs={{0,508},{2,510},{4,0},{6,2},{8,4},{10,6},{12,8},{14,10},{16,12},{1... | collective-permute-start | bytes 1572872 | tf_op jit(solution)/shard_map/ppermute | solution.py:13
  19.8 18.4 %collective-permute-start.4 = (bf16[256,1024]{1,0:T(8,128)(2,1)}, bf16[256,1024]{1,0:T(8,128)(2,1)}, u32[]{:S(2)}, u32[]{:S(2)}) collective-permute-start(bf16[256,1024]{1,0:T(8,128)(2,1)} %bitcast.57), channel_id=1, source_target_pairs={{0,506},{2,0},{4,510},{6,4},{8,2},{10,8},{12,6},{14,12},{16,10},{1... | collective-permute-start | bytes 1572872 | tf_op jit(solution)/shard_map/ppermute | solution.py:22
  23.9 4.0 %copy-start.1 = (bf16[1,256,1024]{2,1,0:T(8,128)(2,1)S(1)}, bf16[1,256,1024]{2,1,0:T(8,128)(2,1)}, u32[]{:S(2)}) copy-start(bf16[1,256,1024]{2,1,0:T(8,128)(2,1)} %param.6) | copy-start | bytes 1572868
  23.9 4.0 %copy-start.9 = (s32[1,256]{1,0:T(1,128)S(1)}, s32[1,256]{1,0:T(1,128)}, u32[]{:S(2)}) copy-start(s32[1,256]{1,0:T(1,128)} %param.9) | copy-start | bytes 3076
  29.4 0.7 copy-start.7
  31.4 15.3 %collective-permute-start.5 = (bf16[256,1024]{1,0:T(8,128)(2,1)}, bf16[256,1024]{1,0:T(8,128)(2,1)}, u32[]{:S(2)}, u32[]{:S(2)}) collective-permute-start(bf16[256,1024]{1,0:T(8,128)(2,1)} %collective-permute-done.3), channel_id=1, source_target_pairs={{0,2},{2,0},{1,3},{3,1},{4,6},{6,4},{5,7},{7,5},{8,10},{10,8},{9,1... | collective-permute-start | bytes 1572872 | tf_op jit(solution)/shard_map/ppermute | solution.py:17
  51.5 2.4 %copy-start.3 = (bf16[1,256,768]{2,1,0:T(8,128)(2,1)S(1)}, bf16[1,256,768]{2,1,0:T(8,128)(2,1)}, u32[]{:S(2)}) copy-start(bf16[1,256,768]{2,1,0:T(8,128)(2,1)} %param.7) | copy-start | bytes 1179652
  51.5 10.8 %copy-start.2 = (bf16[256,1024]{1,0:T(8,128)(2,1)S(1)}, bf16[256,1024]{1,0:T(8,128)(2,1)}, u32[]{:S(2)}) copy-start(bf16[256,1024]{1,0:T(8,128)(2,1)} %multiply_convert_fusion.4) | copy-start | bytes 1572868
  51.5 10.8 %copy-start.8 = (bf16[256,256]{1,0:T(8,128)(2,1)S(1)}, bf16[256,256]{1,0:T(8,128)(2,1)}, u32[]{:S(2)}) copy-start(bf16[256,256]{1,0:T(8,128)(2,1)} %copy-done.7) | copy-start | bytes 393220
  53.1 0.8 copy-start.4
  55.2 14.6 %collective-permute-start.6 = (bf16[768,512]{0,1:T(8,128)(2,1)}, bf16[768,512]{0,1:T(8,128)(2,1)}, u32[]{:S(2)}, u32[]{:S(2)}) collective-permute-start(bf16[768,512]{0,1:T(8,128)(2,1)} %fusion.4), channel_id=1, source_target_pairs={{0,2},{2,0},{1,3},{3,1},{4,6},{6,4},{5,7},{7,5},{8,10},{10,8},{9,1... | collective-permute-start | bytes 2359304 | tf_op jit(solution)/shard_map/ppermute | solution.py:17
  63.6 70.8 %collective-permute-start.2 = (bf16[256,768]{1,0:T(8,128)(2,1)}, bf16[256,768]{1,0:T(8,128)(2,1)}, u32[]{:S(2)}, u32[]{:S(2)}) collective-permute-start(bf16[256,768]{1,0:T(8,128)(2,1)} %collective-permute-done), channel_id=1, source_target_pairs={{0,2},{2,0},{1,3},{3,1},{4,6},{6,4},{5,7},{7,5},{8,10},{10,8},{9,1... | collective-permute-start | bytes 1179656 | tf_op jit(solution)/shard_map/ppermute | solution.py:17
  68.1 1.7 %copy-start.5 = (bf16[256,1024]{1,0:T(8,128)(2,1)S(1)}, bf16[256,1024]{1,0:T(8,128)(2,1)}, u32[]{:S(2)}) copy-start(bf16[256,1024]{1,0:T(8,128)(2,1)} %copy-done.4) | copy-start | bytes 1572868
  74.6 17.7 %all-to-all-start = ((bf16[16,48,512]{2,1,0:T(8,128)(2,1)}), bf16[16,48,512]{2,1,0:T(8,128)(2,1)}, u32[]{:S(2)}, u32[]{:S(2)}) async-start(bf16[16,48,512]{2,1,0:T(8,128)(2,1)} %bitcast.60), calls=%async_computation | async-start | bytes 1572864 | tf_op jit(solution)/shard_map/all_to_all | solution.py:97
  126.2 15.5 %all-to-all-start.1 = ((bf16[16,48,512]{2,1,0:T(8,128)(2,1)}), bf16[16,48,512]{2,1,0:T(8,128)(2,1)}, u32[]{:S(2)}, u32[]{:S(2)}) async-start(bf16[16,48,512]{2,1,0:T(8,128)(2,1)} %broadcast_in_dim.8), calls=%async_computation.1 | async-start | bytes 1572864 | tf_op jit(solution)/shard_map/all_to_all | solution.py:101
  141.8 18.5 %collective-permute-start.7 = (bf16[768,512]{1,0:T(8,128)(2,1)}, bf16[768,512]{1,0:T(8,128)(2,1)}, u32[]{:S(2)}, u32[]{:S(2)}) collective-permute-start(bf16[768,512]{1,0:T(8,128)(2,1)} %bitcast.9), channel_id=1, source_target_pairs={{0,2},{2,0},{1,3},{3,1},{4,6},{6,4},{5,7},{7,5},{8,10},{10,8},{9,1... | collective-permute-start | bytes 2359304 | tf_op jit(solution)/shard_map/ppermute | solution.py:17
  156.6 2.3 %copy-start.6 = (bf16[256,1024]{1,0:T(8,128)(2,1)S(1)}, bf16[256,1024]{1,0:T(8,128)(2,1)}, u32[]{:S(2)}) copy-start(bf16[256,1024]{1,0:T(8,128)(2,1)} %copy-done.4) | copy-start | bytes 1572868

commit v2 on v1

v2 whole, which is shorter than its diff:
```python
import jax
import jax.numpy as jnp
from jax import lax
from jax.experimental import pallas as pl
from jax.experimental.pallas import tpu as pltpu
from jax.sharding import Mesh, PartitionSpec as P

EPS = 1e-06
BLK = ("yl", "x", "zh", "zl", "c")
PLANE = ("yl", "x", "yh")
F32, BF16 = jnp.float32, jnp.bfloat16


def shifted(value, steps):
    count = lax.axis_size(BLK)
    return lax.ppermute(value, BLK, [(i, (i + steps) % count) for i in range(count)])


def other_core(value):
    return lax.ppermute(value, "c", [(0, 1), (1, 0)])


def tied(*values):
    return lax.optimization_barrier(values)


def unit_rows(wide):
    inverse = lax.rsqrt(jnp.sum(wide * wide, axis=-1, keepdims=True) + EPS)
    return (wide * inverse, inverse)


def dot(a, b, da, db):
    return lax.dot_general(a, b, (((da,), (db,)), ((), ())), preferred_element_type=F32)


def tangent(unit, inverse, grad):
    return (grad - unit * jnp.sum(unit * grad, axis=-1, keepdims=True)) * inverse


def sigmoids(left, right, scale, bias):
    return jax.nn.sigmoid(scale * dot(left, right, 1, 1) + bias)


def own_kernel(
    scale_ref, bias_ref, first_ref, audio_ref, feats_ref, head_ref, ident_ref,
    audio_b_ref, text_b_ref, unit_ref, inv_ref, audio_grad_ref, text_grad_ref, turned_ref,
):
    scale, bias = scale_ref[0], bias_ref[0]
    audio_b = unit_rows(audio_ref[...].astype(F32))[0].astype(BF16)
    unit, inverse = unit_rows(dot(feats_ref[...], head_ref[...], 1, 0))
    text_b = unit.astype(BF16)
    rows = audio_b.shape[0]
    owners = first_ref[0] + lax.broadcasted_iota(jnp.int32, (rows, rows), 0)
    positive = (owners == ident_ref[...]).astype(F32)
    weights = scale * (sigmoids(audio_b, text_b, scale, bias) - positive)
    audio_b_ref[...] = audio_b
    text_b_ref[...] = text_b
    unit_ref[...] = unit
    inv_ref[...] = inverse
    audio_grad_ref[...] = dot(weights.astype(BF16), text_b, 1, 0)
    text_grad_ref[...] = dot(weights.T.astype(BF16), audio_b, 1, 0)
    turned_ref[...] = feats_ref[...].T


def column_half(core, value):
    half = value.shape[1] // 2
    return jnp.where(core == 0, value[:, :half], value[:, half:])


def near_kernel(
    scale_ref, bias_ref, core_ref, audio_b_ref, text_b_ref, unit_ref, inv_ref, grad_ref, turned_ref,
    audio_1_ref, feats_2_ref, head_ref,
    proj_grad_ref, proj_grad_2_ref, turned_2_ref, theirs_ref, text_2_ref,
    weights_01_ref, weights_20_ref, weights_21_ref,
):
    scale, bias = scale_ref[0], bias_ref[0]
    audio_0, text_0 = audio_b_ref[...], text_b_ref[...]
    audio_1 = unit_rows(audio_1_ref[...].astype(F32))[0].astype(BF16)
    unit_2, inverse_2 = unit_rows(dot(feats_2_ref[...], head_ref[...], 1, 0))
    text_2 = unit_2.astype(BF16)
    weights_01 = (scale * sigmoids(text_0, audio_1, scale, bias)).astype(BF16)
    weights_20 = (scale * sigmoids(text_2, audio_0, scale, bias)).astype(BF16)
    weights_21 = (scale * sigmoids(text_2, audio_1, scale, bias)).astype(BF16)
    grad_0 = grad_ref[...] + dot(weights_01, audio_1, 1, 0)
    grad_2 = dot(weights_20, audio_0, 1, 0) + dot(weights_21, audio_1, 1, 0)
    proj_grad = tangent(unit_ref[...], inv_ref[...], grad_0).astype(BF16)
    proj_grad_2 = tangent(unit_2, inverse_2, grad_2).astype(BF16)
    turned_2 = feats_2_ref[...].T
    other = 1 - core_ref[0]
    theirs = dot(turned_ref[...], column_half(other, proj_grad), 1, 0)
    theirs += dot(turned_2, column_half(other, proj_grad_2), 1, 0)
    proj_grad_ref[...] = proj_grad
    proj_grad_2_ref[...] = proj_grad_2
    turned_2_ref[...] = turned_2
    theirs_ref[...] = theirs.astype(BF16)
    text_2_ref[...] = text_2
    weights_01_ref[...] = weights_01
    weights_20_ref[...] = weights_20
    weights_21_ref[...] = weights_21


def mine_kernel(core_ref, turned_ref, turned_2_ref, proj_grad_ref, proj_grad_2_ref, out_ref):
    out_ref[...] = dot(turned_ref[...], column_half(core_ref[0], proj_grad_ref[...]), 1, 0) + dot(
        turned_2_ref[...], column_half(core_ref[0], proj_grad_2_ref[...]), 1, 0
    )


def add_kernel(mine_ref, theirs_ref, out_ref):
    total = mine_ref[...] + theirs_ref[...].astype(F32)
    out_ref[...] = total.astype(BF16).reshape(out_ref.shape)


def back_kernel(
    audio_ref, audio_1_ref, grad_ref, text_0_ref, text_2_ref, weights_01_ref, weights_20_ref,
    weights_21_ref, proj_grad_2_ref, head_ref, kept_ref, back_1_ref, back_2_ref,
):
    text_0, text_2 = text_0_ref[...], text_2_ref[...]
    grad_0 = grad_ref[...] + dot(weights_20_ref[...], text_2, 0, 0)
    grad_1 = dot(weights_01_ref[...], text_0, 0, 0) + dot(weights_21_ref[...], text_2, 0, 0)
    kept_ref[...] = tangent(*unit_rows(audio_ref[...].astype(F32)), grad_0)
    back_1_ref[...] = tangent(*unit_rows(audio_1_ref[...].astype(F32)), grad_1).astype(BF16)
    back_2_ref[...] = dot(proj_grad_2_ref[...], head_ref[...], 1, 1).astype(BF16)


def finish_kernel(
    kept_ref, came_1_ref, proj_grad_ref, head_ref, came_2_ref, audio_out_ref, feats_out_ref
):
    audio_out_ref[...] = (kept_ref[...] + came_1_ref[...].astype(F32)).astype(BF16)
    feats = dot(proj_grad_ref[...], head_ref[...], 1, 1) + came_2_ref[...].astype(F32)
    feats_out_ref[...] = feats.astype(BF16)


def spread_kernel(tiles_ref, out_ref):
    total = jnp.sum(tiles_ref[...].astype(F32), axis=0).astype(BF16)
    out_ref[...] = jnp.broadcast_to(total[None], out_ref.shape)


def join_kernel(core_ref, mine_ref, theirs_ref, out_ref):
    half = mine_ref.shape[1]

    @pl.when(core_ref[0] == 0)
    def _():
        out_ref[:, :half] = mine_ref[...]
        out_ref[:, half:] = theirs_ref[...]

    @pl.when(core_ref[0] != 0)
    def _():
        out_ref[:, :half] = theirs_ref[...]
        out_ref[:, half:] = mine_ref[...]


def run(kernel, scalars, arrays, outs, macs):
    smem = pl.BlockSpec(memory_space=pltpu.SMEM)
    vmem = pl.BlockSpec(memory_space=pltpu.VMEM)
    moved = sum(a.size * a.dtype.itemsize for a in (*arrays, *outs))
    single = len(outs) == 1
    return pl.pallas_call(
        kernel,
        out_shape=outs[0] if single else outs,
        in_specs=[smem] * len(scalars) + [vmem] * len(arrays),
        out_specs=vmem if single else [vmem] * len(outs),
        compiler_params=pltpu.CompilerParams(vmem_limit_bytes=20 * 2**20),
        cost_estimate=pl.CostEstimate(flops=2 * macs, bytes_accessed=moved, transcendentals=0),
    )(*[s.reshape(1) for s in scalars], *arrays)


def shared_sum(tiles, copies):
    return run(spread_kernel, (), (tiles,), [jax.ShapeDtypeStruct((copies, *tiles.shape[1:]), BF16)], 0)


def body(audio_embed, text_feats, text_head, pair_ids, scale, bias):
    audio = audio_embed[0]
    feats = text_feats[0]
    rows, wide = audio.shape
    depth = feats.shape[1]
    half = wide // 2
    core = lax.axis_index("c")
    first_row = lax.axis_index(BLK) * rows
    shape = jax.ShapeDtypeStruct
    square, narrow = shape((rows, wide), BF16), shape((rows, depth), BF16)
    total, part_of = shape((rows, wide), F32), shape((depth, half), BF16)
    turned_of, weights_of = shape((depth, rows), BF16), shape((rows, rows), BF16)
    pair, project = rows * rows * wide, rows * wide * depth

    feats_2 = shifted(feats, 2)
    audio_1 = shifted(audio, -1)
    own_audio, own_text, unit, inverse, audio_grad, text_grad, turned = run(
        own_kernel,
        (scale, bias, first_row),
        (audio, feats, text_head, pair_ids),
        [square, square, total, shape((rows, 1), F32), total, total, turned_of],
        project + 3 * pair,
    )
    proj_grad, proj_grad_2, turned_2, theirs, text_2, *weights = run(
        near_kernel,
        (scale, bias, core),
        (own_audio, own_text, unit, inverse, text_grad, turned, audio_1, feats_2, text_head),
        [square, square, turned_of, part_of, square, weights_of, weights_of, weights_of],
        2 * project + 6 * pair,
    )

    theirs = other_core(theirs)
    mine = run(
        mine_kernel, (core,), (turned, turned_2, proj_grad, proj_grad_2),
        [shape((depth, half), F32)], project,
    )
    kept, back_1, back_2 = run(
        back_kernel, (),
        (audio, audio_1, audio_grad, own_text, text_2, *weights, proj_grad_2, text_head),
        [total, square, narrow], 3 * pair + project,
    )
    theirs, kept, back_1, back_2 = tied(theirs, kept, back_1, back_2)
    plane = lax.axis_size(PLANE)
    part = run(add_kernel, (), (mine, theirs), [shape((plane, depth // plane, half), BF16)], 0)
    part, back_1, back_2 = tied(part, back_1, back_2)
    came_2, came_1 = shifted(back_2, -2), shifted(back_1, 1)
    tiles = lax.all_to_all(part, PLANE, 0, 0, tiled=True)
    tile = shared_sum(tiles, lax.axis_size("zl"))
    came_1, came_2, tile = tied(came_1, came_2, tile)
    tiles = lax.all_to_all(tile, "zl", 0, 0, tiled=True)
    tile = shared_sum(tiles, lax.axis_size("zh"))
    tiles = lax.all_to_all(tile, "zh", 0, 0, tiled=True)
    spread = shared_sum(tiles, plane)
    spread = lax.all_to_all(spread, PLANE, 0, 0, tiled=True).reshape(depth, half)
    other_half = other_core(spread)
    came_1, spread = tied(came_1, spread)
    grad_audio, grad_feats = run(
        finish_kernel, (), (kept, came_1, proj_grad, text_head, came_2), [square, narrow], project
    )
    grad_head = run(join_kernel, (core,), (spread, other_half), [shape((depth, wide), BF16)], 0)
    return (grad_audio[None], grad_feats[None], grad_head)


def solution(mesh):
    fine = Mesh(mesh.devices.reshape(2, 4, 4, 4, 2, 2), ("yl", "x", "zh", "zl", "c", "yh"))
    rows = P("yh", BLK, None)
    return jax.shard_map(
        body,
        mesh=fine,
        in_specs=(rows, rows, P(), P("yh", BLK), P(), P()),
        out_specs=(rows, rows, P()),
        check_vma=False,
    )
```

time: 164 us -> 123 us (0.75)
  matrix products: 37.5 us -> 0 us
  starting transfers between devices: 57.7 us -> 40.7 us
  other arithmetic: 15.1 us -> 0 us
  blocking collectives: 30.4 us -> 44.1 us
  Pallas kernels: 0 us -> 11 us
  local copies, waits for them, and re-layouts: 4.81 us -> 8.83 us
    all_to_all x0 -> x3, blocking collectives: none -> 44.1 us  [the longest x1 19.7 us: body(): tiles = lax.all_to_all(tile, 'zh', 0, 0, tiled=True)]
    dot_general x16 -> x0, matrix products: 37.5 us -> none  [the longest x12 29.9 us: dot(): lax.dot_general(a, b, (((da,), (db,)), ((), ())), preferred_element_type=...]
    all_gather x1 -> x0, blocking collectives: 30.4 us -> none  [body(): line = lax.all_gather(tile, 'z', axis=0)]
    pallas_call x0 -> x10, Pallas kernels: none -> 11 us  [run(): pl.pallas_call(kernel, out_shape=outs[0] if single else outs, in_specs=[s...]
    ppermute x4 -> x2, starting transfers between devices: 26.3 us -> 16.4 us  [other_core(): return lax.ppermute(value, 'c', [(0, 1), (1, 0)])]
    ppermute x2 -> x0, starting transfers between devices: 8.61 us -> none  [even_odd(): lax.ppermute(value, BLK, [(i, (i + (odd if i % 2 else even)) % count) for...]
    reduce_sum x6 -> x0, other arithmetic: 7.4 us -> none  [the longest x4 4.9 us: unit_rows(): inverse = lax.rsqrt(jnp.sum(wide * wide, axis=-1, keepdims=True) + EPS)]
    unnamed x20 -> x24, local copies, waits for them, and re-layouts: 1.49 us -> 8.83 us
  transfers between devices with their start and end apart: 10 -> 7, of which waited for: 2 -> 2; matrix products, arithmetic and copies ran while one was open for 33% -> 0% of each run, Pallas kernels for 0% -> 5%
where the time goes in v2:
time: 123 us; the launch traced here: 122 us
  blocking collectives  44.1 us (36%)
  starting transfers between devices  40.7 us (33%)
  waiting for transfers between devices  15 us (12%)
  Pallas kernels  11 us (9%)
  local copies, waits for them, and re-layouts  8.83 us (7%)
  between operations  2.1 us (2%)
    ppermute x4, starting transfers between devices, shifted(): lax.ppermute(value, BLK, [(i, (i + steps) % count) for i in range(count)])  20.4 us
    all_to_all x1, blocking collectives, body(): tiles = lax.all_to_all(tile, 'zh', 0, 0, tiled=True)  19.7 us
    all_to_all x1, blocking collectives, body(): lax.all_to_all(spread, PLANE, 0, 0, tiled=True).reshape(depth, half)  16.4 us
    ppermute x2, starting transfers between devices, other_core(): return lax.ppermute(value, 'c', [(0, 1), (1, 0)])  16.4 us
    pallas_call x10, Pallas kernels, run(): pl.pallas_call(kernel, out_shape=outs[0] if single else outs, in_specs=[s...  11 us
    all_to_all x1, waiting for transfers between devices, body(): tiles = lax.all_to_all(part, PLANE, 0, 0, tiled=True)  9.67 us
    unnamed x24, local copies, waits for them, and re-layouts  8.83 us
    all_to_all x1, blocking collectives, body(): tiles = lax.all_to_all(tile, 'zl', 0, 0, tiled=True)  8.02 us
  transfers between devices with their start and end apart: 7, of which 2 were waited for; matrix products, arithmetic and copies ran while one was open for 0% of the time, Pallas kernels for 5%

profile of v2, /device:TPU:1, one launch (start us, length us, event | category | flops | bytes accessed | tf_op | source)
XLA Modules:
  0.0 121.8 jit_solution(5751846097236432802)
XLA Ops:
  0.6 8.8 %collective-permute-start = (bf16[256,1024]{1,0:T(8,128)(2,1)}, bf16[256,1024]{1,0:T(8,128)(2,1)S(1)}, u32[]{:S(2)}, u32[]{:S(2)}) collective-permute-start(bf16[256,1024]{1,0:T(8,128)(2,1)} %bitcast.15), channel_id=1, source_target_pairs={{0,510},{2,0},{4,2},{6,4},{8,6},{10,8},{12,10},{14,12},{16,14},{18... | collective-permute-start | bytes 1572872 | tf_op jit(solution)/shard_map/ppermute | solution.py:16
  9.4 1.9 %collective-permute-start.1 = (bf16[256,768]{1,0:T(8,128)(2,1)}, bf16[256,768]{1,0:T(8,128)(2,1)S(1)}, u32[]{:S(2)}, u32[]{:S(2)}) collective-permute-start(bf16[256,768]{1,0:T(8,128)(2,1)} %bitcast.18), channel_id=1, source_target_pairs={{0,4},{2,6},{4,8},{6,10},{8,12},{10,14},{12,16},{14,18},{16,20},{1... | collective-permute-start | bytes 1179656 | tf_op jit(solution)/shard_map/ppermute | solution.py:16
  12.7 1.4 %copy-done = bf16[768,1024]{1,0:T(8,128)(2,1)S(1)} copy-done((bf16[768,1024]{1,0:T(8,128)(2,1)S(1)}, bf16[768,1024]{1,0:T(8,128)(2,1)}, u32[]{:S(2)}) %copy-start) | copy-done | bytes 1572888
  14.1 1.0 copy-done.4
  15.1 1.0 copy-done.9
  16.1 0.7 copy-done.11
  16.8 1.6 %shard_map.85 = (bf16[256,1024]{1,0:T(8,128)(2,1)S(1)}, bf16[256,1024]{1,0:T(8,128)(2,1)S(1)}, f32[256,1024]{1,0:T(8,128)S(1)}, f32[256,1]{1,0:T(8,128)S(1)}, f3...) custom-call(f32[1]{0:T(128)} %bitcast.9.scale_ref, f32[1]{0:T(128)} %bitcast.11.bias_ref, ...), custom_call_target="tpu_custom_call" | custom-call | flops 805306368 | bytes 7079936 | tf_op jit(solution)/shard_map/pallas_call | solution.py:157
  18.4 5.3 %collective-permute-done.1.feats_2_ref = bf16[256,768]{1,0:T(8,128)(2,1)S(1)} collective-permute-done((bf16[256,768]{1,0:T(8,128)(2,1)}, bf16[256,768]{1,0:T(8,128)(2,1)S(1)}, u32[]{:S(2)}, u32[]{:S(2)}) %collective-permute-start.1) | collective-permute-done | bytes 393248 | tf_op jit(solution)/shard_map/ppermute | solution.py:16
  23.8 0.7 copy-done.6
  24.5 1.0 copy-done.7
  25.5 2.4 %shard_map.86 = (bf16[256,1024]{1,0:T(8,128)(2,1)S(1)}, bf16[256,1024]{1,0:T(8,128)(2,1)S(1)}, bf16[768,256]{1,0:T(8,128)(2,1)S(1)}, bf16[768,512]{1,0:T(8,128)(...) custom-call(f32[1]{0:T(128)} %bitcast.10.scale_ref, ...), custom_call_target="tpu_custom_call" | custom-call | flops 1610612736 | bytes 9176064 | tf_op jit(solution)/shard_map/pallas_call | solution.py:157
  27.9 8.4 %collective-permute-start.2 = (bf16[768,512]{1,0:T(8,128)(2,1)S(1)}, bf16[768,512]{1,0:T(8,128)(2,1)S(1)}, u32[]{:S(2)}, u32[]{:S(2)}) collective-permute-start(bf16[768,512]{1,0:T(8,128)(2,1)S(1)} %get-tuple-element.41), channel_id=1, source_target_pairs={{0,2},{2,0},{1,3},{3,1},{4,6},{6,4},{5,7},{7,5},{8,10},{10,8},{9,1... | collective-permute-start | bytes 2359304 | tf_op jit(solution)/shard_map/ppermute | solution.py:20
  36.4 0.0 copy-start.5
  36.4 0.6 shard_map.88.mine_ref
  37.0 0.5 copy-done.5
  37.4 1.3 %shard_map.87 = (f32[256,1024]{1,0:T(8,128)S(1)}, bf16[256,1024]{1,0:T(8,128)(2,1)S(1)}, bf16[256,768]{1,0:T(8,128)(2,1)S(1)}) custom-call(bf16[256,1024]{1,0:T(8,128)(2,1)S(1)} %bitcast.17, bf16[256,1024]{1,0:T(8,128)(2,1)S(1)} %collective-permute-done.audio_1_ref, f32[256,1024]{1,0:T(8,128)S(1)} %get-tuple-element.42.grad_ref, ...), custom_call_target="tpu_custom_call" | custom-call | flops 805306368 | bytes 7602176 | tf_op jit(solution)/shard_map/pallas_call | solution.py:157
  38.8 1.0 copy-done.2
  39.7 0.8 copy-done.8
  40.5 0.7 copy-done.10
  41.3 1.0 shard_map.89
  42.3 4.0 %all-to-all-start = ((bf16[16,48,512]{2,1,0:T(8,128)(2,1)}), bf16[16,48,512]{2,1,0:T(8,128)(2,1)S(1)}, u32[]{:S(2)}, u32[]{:S(2)}) async-start(bf16[16,48,512]{2,1,0:T(8,128)(2,1)} %shard_map.89), calls=%async_computation | async-start | bytes 1572864 | tf_op jit(solution)/shard_map/all_to_all | solution.py:217
  46.3 1.9 %collective-permute-start.3 = (bf16[256,1024]{1,0:T(8,128)(2,1)}, bf16[256,1024]{1,0:T(8,128)(2,1)S(1)}, u32[]{:S(2)}, u32[]{:S(2)}) collective-permute-start(bf16[256,1024]{1,0:T(8,128)(2,1)} %copy-done.8), channel_id=1, source_target_pairs={{0,2},{2,4},{4,6},{6,8},{8,10},{10,12},{12,14},{14,16},{16,18},{18... | collective-permute-start | bytes 1572872 | tf_op jit(solution)/shard_map/ppermute | solution.py:16
  48.2 7.8 %collective-permute-start.4 = (bf16[256,768]{1,0:T(8,128)(2,1)}, bf16[256,768]{1,0:T(8,128)(2,1)}, u32[]{:S(2)}, u32[]{:S(2)}) collective-permute-start(bf16[256,768]{1,0:T(8,128)(2,1)} %copy-done.10), channel_id=1, source_target_pairs={{0,508},{2,510},{4,0},{6,2},{8,4},{10,6},{12,8},{14,10},{16,12},{1... | collective-permute-start | bytes 1179656 | tf_op jit(solution)/shard_map/ppermute | solution.py:16
  56.0 9.7 %all-to-all-done.tiles_ref = bf16[16,48,512]{2,1,0:T(8,128)(2,1)S(1)} async-done(((bf16[16,48,512]{2,1,0:T(8,128)(2,1)}), bf16[16,48,512]{2,1,0:T(8,128)(2,1)S(1)}, u32[]{:S(2)}, u32[]{:S(2)}) %all-to-all-start) | async-done | bytes 786464 | tf_op jit(solution)/shard_map/all_to_all | solution.py:217
  65.7 0.1 shard_map.90
  65.8 8.0 %all_to_all.20.tiles_ref = bf16[4,48,512]{2,1,0:T(8,128)(2,1)S(1)} all-to-all(bf16[4,48,512]{2,1,0:T(8,128)(2,1)S(1)} %shard_map.90), channel_id=1, replica_groups=mesh['yl'=2,'x'=4,'zh'=4,'zl'=4,'c'=2,'yh'=2] {'zl'}, dimensions={0} | all-to-all | bytes 393216 | tf_op jit(solution)/shard_map/all_to_all | solution.py:220
  73.9 19.7 %all_to_all.21.tiles_ref = bf16[4,48,512]{2,1,0:T(8,128)(2,1)S(1)} all-to-all(bf16[4,48,512]{2,1,0:T(8,128)(2,1)S(1)} %shard_map.91), channel_id=1, replica_groups=mesh['yl'=2,'x'=4,'zh'=4,'zl'=4,'c'=2,'yh'=2] {'zh'}, dimensions={0} | all-to-all | bytes 393216 | tf_op jit(solution)/shard_map/all_to_all | solution.py:222
  93.5 0.1 shard_map.92
  93.6 16.4 %all_to_all.22 = bf16[16,48,512]{2,1,0:T(8,128)(2,1)S(1)} all-to-all(bf16[16,48,512]{2,1,0:T(8,128)(2,1)S(1)} %shard_map.92), channel_id=1, replica_groups=mesh['yl'=2,'x'=4,'zh'=4,'zl'=4,'c'=2,'yh'=2] {'yl','x','yh'}, dimensions={0} | all-to-all | bytes 1572864 | tf_op jit(solution)/shard_map/all_to_all | solution.py:224
  110.0 7.9 %collective-permute-start.5 = (bf16[768,512]{1,0:T(8,128)(2,1)S(1)}, bf16[768,512]{1,0:T(8,128)(2,1)S(1)}, u32[]{:S(2)}, u32[]{:S(2)}) collective-permute-start(bf16[768,512]{1,0:T(8,128)(2,1)S(1)} %bitcast.13), channel_id=1, source_target_pairs={{0,2},{2,0},{1,3},{3,1},{4,6},{6,4},{5,7},{7,5},{8,10},{10,8},{9,1... | collective-permute-start | bytes 2359304 | tf_op jit(solution)/shard_map/ppermute | solution.py:20
  117.9 2.6 %shard_map.93 = (bf16[256,1024]{1,0:T(8,128)(2,1)}, bf16[256,768]{1,0:T(8,128)(2,1)}) custom-call(f32[256,1024]{1,0:T(8,128)S(1)} %copy-done.3, bf16[256,1024]{1,0:T(8,128)(2,1)S(1)} %collective-permute-done.3.came_1_ref, bf16[256,1024]{1,0:T(8,128)(2,1)S(1)} %get-tuple-element.53.proj_grad_ref, bf16[768,1024]{1,0:T(8,128)(2,1)S(1)} %copy-done.1, ...), custom_call_target="tpu_custom_call" | custom-call | flops 402653184 | bytes 4980736 | tf_op jit(solution)/shard_map/pallas_call | solution.py:157
  120.5 1.3 %shard_map.94 = bf16[768,1024]{1,0:T(8,128)(2,1)} custom-call(s32[1]{0:T(128)} %bitcast.2.core_ref, bf16[768,512]{1,0:T(8,128)(2,1)S(1)} %bitcast.14, bf16[768,512]{1,0:T(8,128)(2,1)S(1)} %collective-permute-done.5.theirs_ref), custom_call_target="tpu_custom_call" | custom-call | bytes 3145728 | tf_op jit(solution)/shard_map/pallas_call | solution.py:157
  (19 shorter events, 0.1 us)
Async XLA Ops:
  0.6 23.9 %collective-permute-start = (bf16[256,1024]{1,0:T(8,128)(2,1)}, bf16[256,1024]{1,0:T(8,128)(2,1)S(1)}, u32[]{:S(2)}, u32[]{:S(2)}) collective-permute-start(bf16[256,1024]{1,0:T(8,128)(2,1)} %bitcast.15), channel_id=1, source_target_pairs={{0,510},{2,0},{4,2},{6,4},{8,6},{10,8},{12,10},{14,12},{16,14},{18... | collective-permute-start | bytes 1572872 | tf_op jit(solution)/shard_map/ppermute | solution.py:16
  9.4 14.3 %collective-permute-start.1 = (bf16[256,768]{1,0:T(8,128)(2,1)}, bf16[256,768]{1,0:T(8,128)(2,1)S(1)}, u32[]{:S(2)}, u32[]{:S(2)}) collective-permute-start(bf16[256,768]{1,0:T(8,128)(2,1)} %bitcast.18), channel_id=1, source_target_pairs={{0,4},{2,6},{4,8},{6,10},{8,12},{10,14},{12,16},{14,18},{16,20},{1... | collective-permute-start | bytes 1179656 | tf_op jit(solution)/shard_map/ppermute | solution.py:16
  12.7 1.4 %copy-start = (bf16[768,1024]{1,0:T(8,128)(2,1)S(1)}, bf16[768,1024]{1,0:T(8,128)(2,1)}, u32[]{:S(2)}) copy-start(bf16[768,1024]{1,0:T(8,128)(2,1)} %head_ref.7) | copy-start | bytes 4718596
  14.1 1.0 copy-start.4
  15.1 1.0 copy-start.9
  16.1 0.7 copy-start.11
  16.8 7.7 %copy-start.1 = (bf16[768,1024]{1,0:T(8,128)(2,1)S(1)}, bf16[768,1024]{1,0:T(8,128)(2,1)}, u32[]{:S(2)}) copy-start(bf16[768,1024]{1,0:T(8,128)(2,1)} %head_ref.7) | copy-start | bytes 4718596
  23.8 0.7 copy-start.6
  24.5 1.0 copy-start.7
  27.9 13.3 %collective-permute-start.2 = (bf16[768,512]{1,0:T(8,128)(2,1)S(1)}, bf16[768,512]{1,0:T(8,128)(2,1)S(1)}, u32[]{:S(2)}, u32[]{:S(2)}) collective-permute-start(bf16[768,512]{1,0:T(8,128)(2,1)S(1)} %get-tuple-element.41), channel_id=1, source_target_pairs={{0,2},{2,0},{1,3},{3,1},{4,6},{6,4},{5,7},{7,5},{8,10},{10,8},{9,1... | collective-permute-start | bytes 2359304 | tf_op jit(solution)/shard_map/ppermute | solution.py:20
  36.4 1.0 copy-start.5
  38.8 1.0 copy-start.2
  39.7 0.8 copy-start.8
  40.5 0.7 copy-start.10
  42.3 23.4 %all-to-all-start = ((bf16[16,48,512]{2,1,0:T(8,128)(2,1)}), bf16[16,48,512]{2,1,0:T(8,128)(2,1)S(1)}, u32[]{:S(2)}, u32[]{:S(2)}) async-start(bf16[16,48,512]{2,1,0:T(8,128)(2,1)} %shard_map.89), calls=%async_computation | async-start | bytes 1572864 | tf_op jit(solution)/shard_map/all_to_all | solution.py:217
  46.3 19.5 %collective-permute-start.3 = (bf16[256,1024]{1,0:T(8,128)(2,1)}, bf16[256,1024]{1,0:T(8,128)(2,1)S(1)}, u32[]{:S(2)}, u32[]{:S(2)}) collective-permute-start(bf16[256,1024]{1,0:T(8,128)(2,1)} %copy-done.8), channel_id=1, source_target_pairs={{0,2},{2,4},{4,6},{6,8},{8,10},{10,12},{12,14},{14,16},{16,18},{18... | collective-permute-start | bytes 1572872 | tf_op jit(solution)/shard_map/ppermute | solution.py:16
  48.2 17.6 %collective-permute-start.4 = (bf16[256,768]{1,0:T(8,128)(2,1)}, bf16[256,768]{1,0:T(8,128)(2,1)}, u32[]{:S(2)}, u32[]{:S(2)}) collective-permute-start(bf16[256,768]{1,0:T(8,128)(2,1)} %copy-done.10), channel_id=1, source_target_pairs={{0,508},{2,510},{4,0},{6,2},{8,4},{10,6},{12,8},{14,10},{16,12},{1... | collective-permute-start | bytes 1179656 | tf_op jit(solution)/shard_map/ppermute | solution.py:16
  73.8 44.0 %copy-start.3 = (f32[256,1024]{1,0:T(8,128)S(1)}, f32[256,1024]{1,0:T(8,128)}, u32[]{:S(2)}) copy-start(f32[256,1024]{1,0:T(8,128)} %copy-done.2) | copy-start | bytes 3145732
  110.0 10.5 %collective-permute-start.5 = (bf16[768,512]{1,0:T(8,128)(2,1)S(1)}, bf16[768,512]{1,0:T(8,128)(2,1)S(1)}, u32[]{:S(2)}, u32[]{:S(2)}) collective-permute-start(bf16[768,512]{1,0:T(8,128)(2,1)S(1)} %bitcast.13), channel_id=1, source_target_pairs={{0,2},{2,0},{1,3},{3,1},{4,6},{6,4},{5,7},{7,5},{8,10},{10,8},{9,1... | collective-permute-start | bytes 2359304 | tf_op jit(solution)/shard_map/ppermute | solution.py:20

commit v3 on v2

v3 whole, which is shorter than its diff:
```python
import jax
import jax.numpy as jnp
from jax import lax
from jax.experimental import pallas as pl
from jax.experimental.pallas import tpu as pltpu
from jax.sharding import Mesh, PartitionSpec as P

EPS = 1e-06
BLK = ("yl", "x", "zh", "zl", "c")
PLANE = ("yl", "x", "yh")
F32, BF16 = jnp.float32, jnp.bfloat16


def shifted(value, steps):
    count = lax.axis_size(BLK)
    return lax.ppermute(value, BLK, [(i, (i + steps) % count) for i in range(count)])


def other_core(value):
    return lax.ppermute(value, "c", [(0, 1), (1, 0)])


def tied(*values):
    return lax.optimization_barrier(values)


def unit_rows(wide):
    inverse = lax.rsqrt(jnp.sum(wide * wide, axis=-1, keepdims=True) + EPS)
    return (wide * inverse, inverse)


def dot(a, b, da, db):
    return lax.dot_general(a, b, (((da,), (db,)), ((), ())), preferred_element_type=F32)


def tangent(unit, inverse, grad):
    return (grad - unit * jnp.sum(unit * grad, axis=-1, keepdims=True)) * inverse


def sigmoids(left, right, scale, bias):
    return jax.nn.sigmoid(scale * dot(left, right, 1, 1) + bias)


def own_kernel(
    scale_ref, bias_ref, first_ref, audio_ref, feats_ref, head_ref, ident_ref,
    audio_b_ref, text_b_ref, unit_ref, inv_ref, text_grad_ref, turned_ref, audio_grad_hbm,
    audio_grad_ref, left,
):
    scale, bias = scale_ref[0], bias_ref[0]
    audio_b = unit_rows(audio_ref[...].astype(F32))[0].astype(BF16)
    unit, inverse = unit_rows(dot(feats_ref[...], head_ref[...], 1, 0))
    text_b = unit.astype(BF16)
    rows = audio_b.shape[0]
    owners = first_ref[0] + lax.broadcasted_iota(jnp.int32, (rows, rows), 0)
    positive = (owners == ident_ref[...]).astype(F32)
    weights = scale * (sigmoids(audio_b, text_b, scale, bias) - positive)
    audio_grad_ref[...] = dot(weights.astype(BF16), text_b, 1, 0)
    copy = pltpu.make_async_copy(audio_grad_ref, audio_grad_hbm, left.at[0])
    copy.start()
    audio_b_ref[...] = audio_b
    text_b_ref[...] = text_b
    unit_ref[...] = unit
    inv_ref[...] = inverse
    text_grad_ref[...] = dot(weights.T.astype(BF16), audio_b, 1, 0)
    turned_ref[...] = feats_ref[...].T
    copy.wait()


def column_half(core, value):
    half = value.shape[1] // 2
    return jnp.where(core == 0, value[:, :half], value[:, half:])


def audio_near_kernel(
    scale_ref, bias_ref, audio_1_ref, text_ref, unit_ref, inv_ref, grad_ref,
    audio_1_b_ref, proj_grad_ref, audio_grad_ref, proj_grad_hbm, kept_ref, left,
):
    text_b = text_ref[...]
    audio_1 = unit_rows(audio_1_ref[...].astype(F32))[0].astype(BF16)
    weights = scale_ref[0] * sigmoids(text_b, audio_1, scale_ref[0], bias_ref[0])
    grad = grad_ref[...] + dot(weights.astype(BF16), audio_1, 1, 0)
    proj_grad = tangent(unit_ref[...], inv_ref[...], grad).astype(BF16)
    proj_grad_ref[...] = proj_grad
    kept_ref[...] = proj_grad
    copy = pltpu.make_async_copy(kept_ref, proj_grad_hbm, left.at[0])
    copy.start()
    audio_1_b_ref[...] = audio_1
    audio_grad_ref[...] = dot(weights.T.astype(BF16), text_b, 1, 0)
    copy.wait()


def text_near_kernel(
    scale_ref, bias_ref, core_ref, feats_2_ref, head_ref, audio_0_ref, audio_1_ref,
    turned_ref, proj_grad_ref,
    text_2_ref, proj_grad_2_ref, turned_2_ref, theirs_ref, weights_21_ref,
    text_2_hbm, weights_20_hbm, text_kept_ref, weights_20_ref, left,
):
    scale, bias = scale_ref[0], bias_ref[0]
    audio_0, audio_1 = audio_0_ref[...], audio_1_ref[...]
    unit, inverse = unit_rows(dot(feats_2_ref[...], head_ref[...], 1, 0))
    text_2 = unit.astype(BF16)
    text_2_ref[...] = text_2
    text_kept_ref[...] = text_2
    first = pltpu.make_async_copy(text_kept_ref, text_2_hbm, left.at[0])
    first.start()
    weights_20 = (scale * sigmoids(text_2, audio_0, scale, bias)).astype(BF16)
    weights_20_ref[...] = weights_20
    second = pltpu.make_async_copy(weights_20_ref, weights_20_hbm, left.at[1])
    second.start()
    weights_21 = (scale * sigmoids(text_2, audio_1, scale, bias)).astype(BF16)
    grad = dot(weights_20, audio_0, 1, 0) + dot(weights_21, audio_1, 1, 0)
    proj_grad_2 = tangent(unit, inverse, grad).astype(BF16)
    turned_2 = feats_2_ref[...].T
    other = 1 - core_ref[0]
    theirs = dot(turned_ref[...], column_half(other, proj_grad_ref[...]), 1, 0)
    theirs += dot(turned_2, column_half(other, proj_grad_2), 1, 0)
    theirs_ref[...] = theirs.astype(BF16)
    proj_grad_2_ref[...] = proj_grad_2
    turned_2_ref[...] = turned_2
    weights_21_ref[...] = weights_21
    first.wait()
    second.wait()


def mine_kernel(core_ref, turned_0_ref, turned_2_ref, proj_grad_0_ref, proj_grad_2_ref, out_ref):
    out_ref[...] = dot(turned_0_ref[...], column_half(core_ref[0], proj_grad_0_ref[...]), 1, 0) + dot(
        turned_2_ref[...], column_half(core_ref[0], proj_grad_2_ref[...]), 1, 0
    )


def add_kernel(mine_ref, theirs_ref, out_ref):
    total = mine_ref[...] + theirs_ref[...].astype(F32)
    out_ref[...] = total.astype(BF16).reshape(out_ref.shape)


def back_kernel(
    audio_1_ref, text_2_ref, weights_21_ref, grad_ref, proj_grad_2_ref, head_ref,
    feats_hbm, audio_hbm, feats_ref, audio_ref, left,
):
    feats_ref[...] = dot(proj_grad_2_ref[...], head_ref[...], 1, 1).astype(BF16)
    first = pltpu.make_async_copy(feats_ref, feats_hbm, left.at[0])
    first.start()
    grad = grad_ref[...] + dot(weights_21_ref[...], text_2_ref[...], 0, 0)
    audio_ref[...] = tangent(*unit_rows(audio_1_ref[...].astype(F32)), grad).astype(BF16)
    second = pltpu.make_async_copy(audio_ref, audio_hbm, left.at[1])
    second.start()
    first.wait()
    second.wait()


def settle_kernel(
    audio_ref, grad_ref, weights_20_ref, text_2_ref, proj_grad_ref, head_ref, came_feats_ref,
    feats_out_ref, kept_hbm, kept_ref, left,
):
    grad = grad_ref[...] + dot(weights_20_ref[...], text_2_ref[...], 0, 0)
    kept_ref[...] = tangent(*unit_rows(audio_ref[...].astype(F32)), grad)
    copy = pltpu.make_async_copy(kept_ref, kept_hbm, left.at[0])
    copy.start()
    feats = dot(proj_grad_ref[...], head_ref[...], 1, 1) + came_feats_ref[...].astype(F32)
    feats_out_ref[...] = feats.astype(BF16)
    copy.wait()


def finish_kernel(kept_ref, came_audio_ref, out_ref):
    out_ref[...] = (kept_ref[...] + came_audio_ref[...].astype(F32)).astype(BF16)


def spread_kernel(tiles_ref, out_ref):
    total = jnp.sum(tiles_ref[...].astype(F32), axis=0).astype(BF16)
    out_ref[...] = jnp.broadcast_to(total[None], out_ref.shape)


def join_kernel(core_ref, mine_ref, theirs_ref, out_ref):
    half = mine_ref.shape[1]

    @pl.when(core_ref[0] == 0)
    def _():
        out_ref[:, :half] = mine_ref[...]
        out_ref[:, half:] = theirs_ref[...]

    @pl.when(core_ref[0] != 0)
    def _():
        out_ref[:, :half] = theirs_ref[...]
        out_ref[:, half:] = mine_ref[...]


def in_hbm(value):
    return pltpu.with_memory_space_constraint(value, pltpu.HBM)


def run(kernel, scalars, arrays, outs, macs, writes=0):
    smem = pl.BlockSpec(memory_space=pltpu.SMEM)
    vmem = pl.BlockSpec(memory_space=pltpu.VMEM)
    hbm = pl.BlockSpec(memory_space=pltpu.HBM)
    moved = sum(a.size * a.dtype.itemsize for a in (*arrays, *outs))
    single = len(outs) == 1
    kept = len(outs) - writes
    scratch = [pltpu.VMEM(a.shape, a.dtype) for a in outs[kept:]]
    if writes:
        scratch.append(pltpu.SemaphoreType.DMA((writes,)))
    outs = outs[:kept] + [pltpu.HBM(a.shape, a.dtype) for a in outs[kept:]]
    return pl.pallas_call(
        kernel,
        out_shape=outs[0] if single else outs,
        in_specs=[smem] * len(scalars) + [vmem] * len(arrays),
        out_specs=vmem if single else [vmem] * kept + [hbm] * writes,
        scratch_shapes=scratch,
        compiler_params=pltpu.CompilerParams(vmem_limit_bytes=20 * 2**20),
        cost_estimate=pl.CostEstimate(flops=2 * macs, bytes_accessed=moved, transcendentals=0),
    )(*[s.reshape(1) for s in scalars], *arrays)


def shared_sum(tiles, copies):
    return run(spread_kernel, (), (tiles,), [jax.ShapeDtypeStruct((copies, *tiles.shape[1:]), BF16)], 0)


def body(audio_embed, text_feats, text_head, pair_ids, scale, bias):
    audio = audio_embed[0]
    feats = text_feats[0]
    rows, wide = audio.shape
    depth = feats.shape[1]
    half = wide // 2
    core = lax.axis_index("c")
    first_row = lax.axis_index(BLK) * rows
    shape = jax.ShapeDtypeStruct
    square, narrow = shape((rows, wide), BF16), shape((rows, depth), BF16)
    total, part_of = shape((rows, wide), F32), shape((depth, half), BF16)
    turned_of, weights_of = shape((depth, rows), BF16), shape((rows, rows), BF16)
    pair, project = rows * rows * wide, rows * wide * depth

    feats_2 = shifted(feats, 2)
    audio_1 = shifted(audio, -1)
    own_audio, own_text, unit, inverse, text_grad, turned, audio_grad = run(
        own_kernel,
        (scale, bias, first_row),
        tuple(map(in_hbm, (audio, feats, text_head, pair_ids))),
        [square, square, total, shape((rows, 1), F32), total, turned_of, total],
        project + 3 * pair,
        writes=1,
    )
    audio_1_b, proj_grad, audio_1_grad, proj_grad_out = run(
        audio_near_kernel, (scale, bias), (audio_1, own_text, unit, inverse, text_grad),
        [square, square, total, square], 3 * pair, writes=1,
    )
    text_2, proj_grad_2, turned_2, theirs, weights_21, text_2_out, weights_20 = run(
        text_near_kernel, (scale, bias, core),
        (feats_2, text_head, own_audio, audio_1_b, turned, proj_grad),
        [square, square, turned_of, part_of, weights_of, square, weights_of],
        2 * project + 4 * pair, writes=2,
    )

    theirs = other_core(theirs)
    mine = run(
        mine_kernel, (core,), (turned, turned_2, proj_grad, proj_grad_2),
        [shape((depth, half), F32)], project,
    )
    back_feats, back_audio = run(
        back_kernel, (),
        (audio_1, text_2, weights_21, audio_1_grad, proj_grad_2, text_head),
        [narrow, square], pair + project, writes=2,
    )
    theirs, back_audio, back_feats = tied(theirs, back_audio, back_feats)
    plane = lax.axis_size(PLANE)
    part = run(add_kernel, (), (mine, theirs), [shape((plane, depth // plane, half), BF16)], 0)
    part, back_audio, back_feats = tied(part, back_audio, back_feats)
    came_audio, came_feats = shifted(back_audio, 1), shifted(back_feats, -2)
    tiles = lax.all_to_all(part, PLANE, 0, 0, tiled=True)
    tile = shared_sum(tiles, lax.axis_size("zl"))
    came_audio, came_feats, tile = tied(came_audio, came_feats, tile)
    tiles = lax.all_to_all(tile, "zl", 0, 0, tiled=True)
    tile = shared_sum(tiles, lax.axis_size("zh"))
    came_feats, tile = tied(came_feats, tile)
    grad_feats, kept = run(
        settle_kernel, (),
        tuple(map(in_hbm, (audio, audio_grad, weights_20, text_2_out, proj_grad_out, text_head,
                           came_feats))),
        [narrow, total], pair + project, writes=1,
    )
    tiles = lax.all_to_all(tile, "zh", 0, 0, tiled=True)
    tiles, grad_feats, kept = tied(tiles, grad_feats, kept)
    spread = shared_sum(tiles, plane)
    spread = lax.all_to_all(spread, PLANE, 0, 0, tiled=True).reshape(depth, half)
    other_half = other_core(spread)
    grad_audio = run(finish_kernel, (), (in_hbm(kept), in_hbm(came_audio)), [square], 0)
    grad_head = run(join_kernel, (core,), (spread, other_half), [shape((depth, wide), BF16)], 0)
    return (grad_audio[None], grad_feats[None], grad_head)


def solution(mesh):
    fine = Mesh(mesh.devices.reshape(2, 4, 4, 4, 2, 2), ("yl", "x", "zh", "zl", "c", "yh"))
    rows = P("yh", BLK, None)
    return jax.shard_map(
        body,
        mesh=fine,
        in_specs=(rows, rows, P(), P("yh", BLK), P(), P()),
        out_specs=(rows, rows, P()),
        check_vma=False,
    )
```

time: 123 us -> 118 us (0.959)
  blocking collectives: 44.1 us -> 26.3 us
  Pallas kernels: 11 us -> 21 us
  local copies, waits for them, and re-layouts: 8.83 us -> 0.03 us
  waiting for transfers between devices: 15 us -> 22.6 us
  starting transfers between devices: 40.7 us -> 45 us
    all_to_all x1 -> x0, blocking collectives: 19.7 us -> none  [body(): tiles = lax.all_to_all(tile, 'zh', 0, 0, tiled=True)]
    pallas_call x10 -> x12, Pallas kernels: 11 us -> 21 us  [run(): pl.pallas_call(kernel, out_shape=outs[0] if single else outs, in_specs=[s...]
    unnamed x24 -> x10, local copies, waits for them, and re-layouts: 8.83 us -> 0.03 us
    all_to_all x0 -> x1, waiting for transfers between devices: none -> 7.83 us  [body(): tiles = lax.all_to_all(tile, 'zh', 0, 0, tiled=True)]
    all_to_all x0 -> x1, starting transfers between devices: none -> 5.02 us  [body(): tiles = lax.all_to_all(tile, 'zh', 0, 0, tiled=True)]
    all_to_all x1, blocking collectives: 16.4 us -> 18.3 us  [body(): lax.all_to_all(spread, PLANE, 0, 0, tiled=True).reshape(depth, half)]
  transfers between devices with their start and end apart: 7 -> 8, of which waited for: 2 -> 3; matrix products, arithmetic and copies ran while one was open for 0% -> 0% of each run, Pallas kernels for 5% -> 13%
where the time goes in v3:
time: 118 us; the launch traced here: 117 us
  starting transfers between devices  45 us (38%)
  blocking collectives  26.3 us (22%)
  waiting for transfers between devices  22.6 us (19%)
  Pallas kernels  21 us (18%)
  between operations  2.15 us (2%)
    pallas_call x12, Pallas kernels, run(): pl.pallas_call(kernel, out_shape=outs[0] if single else outs, in_specs=[s...  21 us
    ppermute x4, starting transfers between devices, shifted(): lax.ppermute(value, BLK, [(i, (i + steps) % count) for i in range(count)])  20.4 us
    all_to_all x1, blocking collectives, body(): lax.all_to_all(spread, PLANE, 0, 0, tiled=True).reshape(depth, half)  18.3 us
    ppermute x2, starting transfers between devices, other_core(): return lax.ppermute(value, 'c', [(0, 1), (1, 0)])  15.6 us
    all_to_all x1, waiting for transfers between devices, body(): tiles = lax.all_to_all(part, PLANE, 0, 0, tiled=True)  9.79 us
    all_to_all x1, blocking collectives, body(): tiles = lax.all_to_all(tile, 'zl', 0, 0, tiled=True)  8.03 us
    all_to_all x1, waiting for transfers between devices, body(): tiles = lax.all_to_all(tile, 'zh', 0, 0, tiled=True)  7.83 us
    all_to_all x1, starting transfers between devices, body(): tiles = lax.all_to_all(tile, 'zh', 0, 0, tiled=True)  5.02 us
  transfers between devices with their start and end apart: 8, of which 3 were waited for; matrix products, arithmetic and copies ran while one was open for 0% of the time, Pallas kernels for 13%

profile of v3, /device:TPU:1, one launch (start us, length us, event | category | flops | bytes accessed | tf_op | source)
XLA Modules:
  0.0 117.1 jit_solution(6584420043651104332)
XLA Ops:
  0.6 8.8 %collective-permute-start.1 = (bf16[256,1024]{1,0:T(8,128)(2,1)}, bf16[256,1024]{1,0:T(8,128)(2,1)S(1)}, u32[]{:S(2)}, u32[]{:S(2)}) collective-permute-start(bf16[256,1024]{1,0:T(8,128)(2,1)} %bitcast.17), channel_id=1, source_target_pairs={{0,510},{2,0},{4,2},{6,4},{8,6},{10,8},{12,10},{14,12},{16,14},{18... | collective-permute-start | bytes 1572872 | tf_op jit(solution)/shard_map/ppermute | solution.py:16
  9.4 1.9 %collective-permute-start = (bf16[256,768]{1,0:T(8,128)(2,1)}, bf16[256,768]{1,0:T(8,128)(2,1)S(1)}, u32[]{:S(2)}, u32[]{:S(2)}) collective-permute-start(bf16[256,768]{1,0:T(8,128)(2,1)} %bitcast.21), channel_id=1, source_target_pairs={{0,4},{2,6},{4,8},{6,10},{8,12},{10,14},{12,16},{14,18},{16,20},{1... | collective-permute-start | bytes 1179656 | tf_op jit(solution)/shard_map/ppermute | solution.py:16
  12.7 4.2 %shard_map.85 = (bf16[256,1024]{1,0:T(8,128)(2,1)S(1)}, bf16[256,1024]{1,0:T(8,128)(2,1)S(1)}, f32[256,1024]{1,0:T(8,128)S(1)}, f32[256,1]{1,0:T(8,128)S(1)}, f3...) custom-call(f32[1]{0:T(128)} %bitcast.9.scale_ref, f32[1]{0:T(128)} %bitcast.12.bias_ref, ...), custom_call_target="tpu_custom_call" | custom-call | flops 805306368 | bytes 7079936 | tf_op jit(solution)/shard_map/pallas_call | solution.py:202
  16.8 0.0 collective-permute-done.1.audio_1_ref
  16.9 0.0 copy-start
  16.9 1.9 %shard_map.86 = (bf16[256,1024]{1,0:T(8,128)(2,1)S(1)}, bf16[256,1024]{1,0:T(8,128)(2,1)S(1)}, f32[256,1024]{1,0:T(8,128)S(1)}, bf16[256,1024]{1,0:T(8,128)(2,1)}) custom-call(f32[1]{0:T(128)} %bitcast.10.scale_ref, f32[1]{0:T(128)} %bitcast.13.bias_ref, bf16[256,1024]{1,0:T(8,128)(2,1)S(1)} %collective-permute-done.1.audio_1_ref, ...), custom_call_target="tpu_custom_call" | custom-call | flops 402653184 | bytes 5768192 | tf_op jit(solution)/shard_map/pallas_call | solution.py:202
  18.8 4.9 %collective-permute-done.feats_2_ref = bf16[256,768]{1,0:T(8,128)(2,1)S(1)} collective-permute-done((bf16[256,768]{1,0:T(8,128)(2,1)}, bf16[256,768]{1,0:T(8,128)(2,1)S(1)}, u32[]{:S(2)}, u32[]{:S(2)}) %collective-permute-start) | collective-permute-done | bytes 393248 | tf_op jit(solution)/shard_map/ppermute | solution.py:16
  23.8 2.3 %shard_map.87 = (bf16[256,1024]{1,0:T(8,128)(2,1)S(1)}, bf16[256,1024]{1,0:T(8,128)(2,1)S(1)}, bf16[768,256]{1,0:T(8,128)(2,1)S(1)}, bf16[768,512]{1,0:T(8,128)(...) custom-call(f32[1]{0:T(128)} %bitcast.11.scale_ref, ...), custom_call_target="tpu_custom_call" | custom-call | flops 1342177280 | bytes 6946816 | tf_op jit(solution)/shard_map/pallas_call | solution.py:202
  26.1 8.4 %collective-permute-start.2 = (bf16[768,512]{1,0:T(8,128)(2,1)S(1)}, bf16[768,512]{1,0:T(8,128)(2,1)S(1)}, u32[]{:S(2)}, u32[]{:S(2)}) collective-permute-start(bf16[768,512]{1,0:T(8,128)(2,1)S(1)} %get-tuple-element.49), channel_id=1, source_target_pairs={{0,2},{2,0},{1,3},{3,1},{4,6},{6,4},{5,7},{7,5},{8,10},{10,8},{9,1... | collective-permute-start | bytes 2359304 | tf_op jit(solution)/shard_map/ppermute | solution.py:20
  34.6 0.6 shard_map.88.mine_ref
  35.1 1.8 %shard_map.89 = (bf16[256,768]{1,0:T(8,128)(2,1)}, bf16[256,1024]{1,0:T(8,128)(2,1)}) custom-call(bf16[256,1024]{1,0:T(8,128)(2,1)S(1)} %collective-permute-done.1.audio_1_ref, bf16[256,1024]{1,0:T(8,128)(2,1)S(1)} %get-tuple-element.50.text_2_ref, bf16[256,256]{1,0:T(8,128)(2,1)S(1)} %get-tuple-element.51.weights_21_ref, ...), custom_call_target="tpu_custom_call" | custom-call | flops 536870912 | bytes 5242880 | tf_op jit(solution)/shard_map/pallas_call | solution.py:202
  37.0 0.0 collective-permute-done.2.theirs_ref
  37.0 0.0 copy-start.4
  37.0 1.0 shard_map.90
  38.0 4.0 %all-to-all-start = ((bf16[16,48,512]{2,1,0:T(8,128)(2,1)}), bf16[16,48,512]{2,1,0:T(8,128)(2,1)S(1)}, u32[]{:S(2)}, u32[]{:S(2)}) async-start(bf16[16,48,512]{2,1,0:T(8,128)(2,1)} %shard_map.90), calls=%async_computation | async-start | bytes 1572864 | tf_op jit(solution)/shard_map/all_to_all | solution.py:267
  42.0 1.9 %collective-permute-start.3 = (bf16[256,1024]{1,0:T(8,128)(2,1)S(1)}, bf16[256,1024]{1,0:T(8,128)(2,1)S(1)}, u32[]{:S(2)}, u32[]{:S(2)}) collective-permute-start(bf16[256,1024]{1,0:T(8,128)(2,1)S(1)} %copy-done.3), channel_id=1, source_target_pairs={{0,2},{2,4},{4,6},{6,8},{8,10},{10,12},{12,14},{14,16},{16,18},{18... | collective-permute-start | bytes 1572872 | tf_op jit(solution)/shard_map/ppermute | solution.py:16
  44.0 7.8 %collective-permute-start.4 = (bf16[256,768]{1,0:T(8,128)(2,1)S(1)}, bf16[256,768]{1,0:T(8,128)(2,1)S(1)}, u32[]{:S(2)}, u32[]{:S(2)}) collective-permute-start(bf16[256,768]{1,0:T(8,128)(2,1)S(1)} %copy-done.4), channel_id=1, source_target_pairs={{0,508},{2,510},{4,0},{6,2},{8,4},{10,6},{12,8},{14,10},{16,12},{1... | collective-permute-start | bytes 1179656 | tf_op jit(solution)/shard_map/ppermute | solution.py:16
  51.7 9.8 %all-to-all-done.tiles_ref = bf16[16,48,512]{2,1,0:T(8,128)(2,1)S(1)} async-done(((bf16[16,48,512]{2,1,0:T(8,128)(2,1)}), bf16[16,48,512]{2,1,0:T(8,128)(2,1)S(1)}, u32[]{:S(2)}, u32[]{:S(2)}) %all-to-all-start) | async-done | bytes 786464 | tf_op jit(solution)/shard_map/all_to_all | solution.py:267
  61.5 0.1 shard_map.91
  61.6 0.0 collective-permute-done.4.came_feats_ref
  61.7 0.0 collective-permute-done.3.came_audio_ref
  61.7 8.0 %all_to_all.20.tiles_ref = bf16[4,48,512]{2,1,0:T(8,128)(2,1)S(1)} all-to-all(bf16[4,48,512]{2,1,0:T(8,128)(2,1)S(1)} %shard_map.91), channel_id=1, replica_groups=mesh['yl'=2,'x'=4,'zh'=4,'zl'=4,'c'=2,'yh'=2] {'zl'}, dimensions={0} | all-to-all | bytes 393216 | tf_op jit(solution)/shard_map/all_to_all | solution.py:270
  69.7 0.7 shard_map.92
  70.4 5.0 %all-to-all-start.2 = ((bf16[4,48,512]{2,1,0:T(8,128)(2,1)}), bf16[4,48,512]{2,1,0:T(8,128)(2,1)S(1)}, u32[]{:S(2)}, u32[]{:S(2)}) async-start(bf16[4,48,512]{2,1,0:T(8,128)(2,1)} %shard_map.92), calls=%async_computation.2 | async-start | bytes 393216 | tf_op jit(solution)/shard_map/all_to_all | solution.py:279
  75.4 4.7 %shard_map.93 = (bf16[256,768]{1,0:T(8,128)(2,1)}, f32[256,1024]{1,0:T(8,128)}) custom-call(bf16[256,1024]{1,0:T(8,128)(2,1)} %bitcast.19, f32[256,1024]{1,0:T(8,128)} %get-tuple-element.64.grad_ref, bf16[256,256]{1,0:T(8,128)(2,1)} %get-tuple-element.65.weights_20_ref, bf16[256,1024]{1,0:T(8,128)(2,1)} %get-tuple-element.66.text_2_ref, ...), custom_call_target="tpu_custom_call" | custom-call | flops 536870912 | bytes 6160384 | tf_op jit(solution)/shard_map/pallas_call | solution.py:202
  80.2 7.8 %all-to-all-done.2.tiles_ref = bf16[4,48,512]{2,1,0:T(8,128)(2,1)S(1)} async-done(((bf16[4,48,512]{2,1,0:T(8,128)(2,1)}), bf16[4,48,512]{2,1,0:T(8,128)(2,1)S(1)}, u32[]{:S(2)}, u32[]{:S(2)}) %all-to-all-start.2) | async-done | bytes 196640 | tf_op jit(solution)/shard_map/all_to_all | solution.py:279
  88.0 0.1 shard_map.95
  88.1 18.3 %all_to_all.21 = bf16[16,48,512]{2,1,0:T(8,128)(2,1)S(1)} all-to-all(bf16[16,48,512]{2,1,0:T(8,128)(2,1)S(1)} %shard_map.95), channel_id=1, replica_groups=mesh['yl'=2,'x'=4,'zh'=4,'zl'=4,'c'=2,'yh'=2] {'yl','x','yh'}, dimensions={0} | all-to-all | bytes 1572864 | tf_op jit(solution)/shard_map/all_to_all | solution.py:282
  106.4 7.2 %collective-permute-start.5 = (bf16[768,512]{1,0:T(8,128)(2,1)S(1)}, bf16[768,512]{1,0:T(8,128)(2,1)S(1)}, u32[]{:S(2)}, u32[]{:S(2)}) collective-permute-start(bf16[768,512]{1,0:T(8,128)(2,1)S(1)} %bitcast.15), channel_id=1, source_target_pairs={{0,2},{2,0},{1,3},{3,1},{4,6},{6,4},{5,7},{7,5},{8,10},{10,8},{9,1... | collective-permute-start | bytes 2359304 | tf_op jit(solution)/shard_map/ppermute | solution.py:20
  113.6 2.2 %shard_map.94 = bf16[256,1024]{1,0:T(8,128)(2,1)} custom-call(f32[256,1024]{1,0:T(8,128)} %get-tuple-element.71.kept_ref, bf16[256,1024]{1,0:T(8,128)(2,1)} %copy-done.1), custom_call_target="tpu_custom_call" | custom-call | bytes 2097152 | tf_op jit(solution)/shard_map/pallas_call | solution.py:202
  115.8 0.0 collective-permute-done.5.theirs_ref
  115.8 1.3 %shard_map.96 = bf16[768,1024]{1,0:T(8,128)(2,1)} custom-call(s32[1]{0:T(128)} %bitcast.core_ref, bf16[768,512]{1,0:T(8,128)(2,1)S(1)} %bitcast.16, bf16[768,512]{1,0:T(8,128)(2,1)S(1)} %collective-permute-done.5.theirs_ref), custom_call_target="tpu_custom_call" | custom-call | bytes 3145728 | tf_op jit(solution)/shard_map/pallas_call | solution.py:202
  (8 shorter events, 0.0 us)
Async XLA Ops:
  0.6 16.2 %collective-permute-start.1 = (bf16[256,1024]{1,0:T(8,128)(2,1)}, bf16[256,1024]{1,0:T(8,128)(2,1)S(1)}, u32[]{:S(2)}, u32[]{:S(2)}) collective-permute-start(bf16[256,1024]{1,0:T(8,128)(2,1)} %bitcast.17), channel_id=1, source_target_pairs={{0,510},{2,0},{4,2},{6,4},{8,6},{10,8},{12,10},{14,12},{16,14},{18... | collective-permute-start | bytes 1572872 | tf_op jit(solution)/shard_map/ppermute | solution.py:16
  9.4 14.3 %collective-permute-start = (bf16[256,768]{1,0:T(8,128)(2,1)}, bf16[256,768]{1,0:T(8,128)(2,1)S(1)}, u32[]{:S(2)}, u32[]{:S(2)}) collective-permute-start(bf16[256,768]{1,0:T(8,128)(2,1)} %bitcast.21), channel_id=1, source_target_pairs={{0,4},{2,6},{4,8},{6,10},{8,12},{10,14},{12,16},{14,18},{16,20},{1... | collective-permute-start | bytes 1179656 | tf_op jit(solution)/shard_map/ppermute | solution.py:16
  16.9 6.9 %copy-start = (bf16[768,1024]{1,0:T(8,128)(2,1)S(1)}, bf16[768,1024]{1,0:T(8,128)(2,1)}, u32[]{:S(2)}) copy-start(bf16[768,1024]{1,0:T(8,128)(2,1)} %head_ref.7) | copy-start | bytes 4718596
  26.1 10.9 %collective-permute-start.2 = (bf16[768,512]{1,0:T(8,128)(2,1)S(1)}, bf16[768,512]{1,0:T(8,128)(2,1)S(1)}, u32[]{:S(2)}, u32[]{:S(2)}) collective-permute-start(bf16[768,512]{1,0:T(8,128)(2,1)S(1)} %get-tuple-element.49), channel_id=1, source_target_pairs={{0,2},{2,0},{1,3},{3,1},{4,6},{6,4},{5,7},{7,5},{8,10},{10,8},{9,1... | collective-permute-start | bytes 2359304 | tf_op jit(solution)/shard_map/ppermute | solution.py:20
  37.0 5.0 %copy-start.3 = (bf16[256,1024]{1,0:T(8,128)(2,1)S(1)}, bf16[256,1024]{1,0:T(8,128)(2,1)}, u32[]{:S(2)}) copy-start(bf16[256,1024]{1,0:T(8,128)(2,1)} %get-tuple-element.58) | copy-start | bytes 1572868
  37.0 7.0 %copy-start.4 = (bf16[256,768]{1,0:T(8,128)(2,1)S(1)}, bf16[256,768]{1,0:T(8,128)(2,1)}, u32[]{:S(2)}) copy-start(bf16[256,768]{1,0:T(8,128)(2,1)} %get-tuple-element.59) | copy-start | bytes 1179652
  38.0 23.5 %all-to-all-start = ((bf16[16,48,512]{2,1,0:T(8,128)(2,1)}), bf16[16,48,512]{2,1,0:T(8,128)(2,1)S(1)}, u32[]{:S(2)}, u32[]{:S(2)}) async-start(bf16[16,48,512]{2,1,0:T(8,128)(2,1)} %shard_map.90), calls=%async_computation | async-start | bytes 1572864 | tf_op jit(solution)/shard_map/all_to_all | solution.py:267
  42.0 19.6 %collective-permute-start.3 = (bf16[256,1024]{1,0:T(8,128)(2,1)S(1)}, bf16[256,1024]{1,0:T(8,128)(2,1)S(1)}, u32[]{:S(2)}, u32[]{:S(2)}) collective-permute-start(bf16[256,1024]{1,0:T(8,128)(2,1)S(1)} %copy-done.3), channel_id=1, source_target_pairs={{0,2},{2,4},{4,6},{6,8},{8,10},{10,12},{12,14},{14,16},{16,18},{18... | collective-permute-start | bytes 1572872 | tf_op jit(solution)/shard_map/ppermute | solution.py:16
  44.0 17.7 %collective-permute-start.4 = (bf16[256,768]{1,0:T(8,128)(2,1)S(1)}, bf16[256,768]{1,0:T(8,128)(2,1)S(1)}, u32[]{:S(2)}, u32[]{:S(2)}) collective-permute-start(bf16[256,768]{1,0:T(8,128)(2,1)S(1)} %copy-done.4), channel_id=1, source_target_pairs={{0,508},{2,510},{4,0},{6,2},{8,4},{10,6},{12,8},{14,10},{16,12},{1... | collective-permute-start | bytes 1179656 | tf_op jit(solution)/shard_map/ppermute | solution.py:16
  61.6 13.8 %copy-start.2 = (bf16[256,768]{1,0:T(8,128)(2,1)}, bf16[256,768]{1,0:T(8,128)(2,1)S(1)}, u32[]{:S(2)}) copy-start(bf16[256,768]{1,0:T(8,128)(2,1)S(1)} %collective-permute-done.4.came_feats_ref) | copy-start | bytes 1179652
  61.7 18.5 %copy-start.1 = (bf16[256,1024]{1,0:T(8,128)(2,1)}, bf16[256,1024]{1,0:T(8,128)(2,1)S(1)}, u32[]{:S(2)}) copy-start(bf16[256,1024]{1,0:T(8,128)(2,1)S(1)} %collective-permute-done.3.came_audio_ref) | copy-start | bytes 1572868
  70.4 17.6 %all-to-all-start.2 = ((bf16[4,48,512]{2,1,0:T(8,128)(2,1)}), bf16[4,48,512]{2,1,0:T(8,128)(2,1)S(1)}, u32[]{:S(2)}, u32[]{:S(2)}) async-start(bf16[4,48,512]{2,1,0:T(8,128)(2,1)} %shard_map.92), calls=%async_computation.2 | async-start | bytes 393216 | tf_op jit(solution)/shard_map/all_to_all | solution.py:279
  106.4 9.4 %collective-permute-start.5 = (bf16[768,512]{1,0:T(8,128)(2,1)S(1)}, bf16[768,512]{1,0:T(8,128)(2,1)S(1)}, u32[]{:S(2)}, u32[]{:S(2)}) collective-permute-start(bf16[768,512]{1,0:T(8,128)(2,1)S(1)} %bitcast.15), channel_id=1, source_target_pairs={{0,2},{2,0},{1,3},{3,1},{4,6},{6,4},{5,7},{7,5},{8,10},{10,8},{9,1... | collective-permute-start | bytes 2359304 | tf_op jit(solution)/shard_map/ppermute | solution.py:20

commit v4 on v3

--- a/solution.py
+++ b/solution.py
@@ -64,6 +64,10 @@
     text_grad_ref[...] = dot(weights.T.astype(BF16), audio_b, 1, 0)
     turned_ref[...] = feats_ref[...].T
     copy.wait()
+
+
+def joined(low_ref, high_ref):
+    return jnp.concatenate([low_ref[...], high_ref[...]], axis=1).astype(F32)
 
 
 def column_half(core, value):
@@ -122,47 +126,44 @@
     second.wait()
 
 
-def mine_kernel(core_ref, turned_0_ref, turned_2_ref, proj_grad_0_ref, proj_grad_2_ref, out_ref):
-    out_ref[...] = dot(turned_0_ref[...], column_half(core_ref[0], proj_grad_0_ref[...]), 1, 0) + dot(
-        turned_2_ref[...], column_half(core_ref[0], proj_grad_2_ref[...]), 1, 0
-    )
-
-
 def add_kernel(mine_ref, theirs_ref, out_ref):
     total = mine_ref[...] + theirs_ref[...].astype(F32)
     out_ref[...] = total.astype(BF16).reshape(out_ref.shape)
 
 
 def back_kernel(
-    audio_1_ref, text_2_ref, weights_21_ref, grad_ref, proj_grad_2_ref, head_ref,
-    feats_hbm, audio_hbm, feats_ref, audio_ref, left,
-):
-    feats_ref[...] = dot(proj_grad_2_ref[...], head_ref[...], 1, 1).astype(BF16)
+    core_ref, audio_1_ref, text_2_ref, weights_21_ref, grad_ref, head_ref,
+    turned_ref, turned_2_ref, proj_grad_ref, proj_grad_2_ref,
+    mine_ref, feats_hbm, low_hbm, high_hbm, feats_ref, low_ref, high_ref, left,
+):
+    proj_grad_2 = proj_grad_2_ref[...]
+    feats_ref[...] = dot(proj_grad_2, head_ref[...], 1, 1).astype(BF16)
     first = pltpu.make_async_copy(feats_ref, feats_hbm, left.at[0])
     first.start()
     grad = grad_ref[...] + dot(weights_21_ref[...], text_2_ref[...], 0, 0)
-    audio_ref[...] = tangent(*unit_rows(audio_1_ref[...].astype(F32)), grad).astype(BF16)
-    second = pltpu.make_async_copy(audio_ref, audio_hbm, left.at[1])
+    back = tangent(*unit_rows(audio_1_ref[...].astype(F32)), grad).astype(BF16)
+    half = back.shape[1] // 2
+    low_ref[...], high_ref[...] = back[:, :half], back[:, half:]
+    second = pltpu.make_async_copy(low_ref, low_hbm, left.at[1])
     second.start()
+    third = pltpu.make_async_copy(high_ref, high_hbm, left.at[2])
+    third.start()
+    mine = dot(turned_ref[...], column_half(core_ref[0], proj_grad_ref[...]), 1, 0)
+    mine_ref[...] = mine + dot(turned_2_ref[...], column_half(core_ref[0], proj_grad_2), 1, 0)
     first.wait()
     second.wait()
+    third.wait()
 
 
 def settle_kernel(
-    audio_ref, grad_ref, weights_20_ref, text_2_ref, proj_grad_ref, head_ref, came_feats_ref,
-    feats_out_ref, kept_hbm, kept_ref, left,
+    audio_ref, grad_ref, weights_20_ref, text_2_ref, came_low_ref, came_high_ref, proj_grad_ref,
+    head_ref, came_feats_ref, audio_out_ref, feats_out_ref,
 ):
     grad = grad_ref[...] + dot(weights_20_ref[...], text_2_ref[...], 0, 0)
-    kept_ref[...] = tangent(*unit_rows(audio_ref[...].astype(F32)), grad)
-    copy = pltpu.make_async_copy(kept_ref, kept_hbm, left.at[0])
-    copy.start()
+    kept = tangent(*unit_rows(audio_ref[...].astype(F32)), grad)
+    audio_out_ref[...] = (kept + joined(came_low_ref, came_high_ref)).astype(BF16)
     feats = dot(proj_grad_ref[...], head_ref[...], 1, 1) + came_feats_ref[...].astype(F32)
     feats_out_ref[...] = feats.astype(BF16)
-    copy.wait()
-
-
-def finish_kernel(kept_ref, came_audio_ref, out_ref):
-    out_ref[...] = (kept_ref[...] + came_audio_ref[...].astype(F32)).astype(BF16)
 
 
 def spread_kernel(tiles_ref, out_ref):
@@ -250,39 +251,38 @@
     )
 
     theirs = other_core(theirs)
-    mine = run(
-        mine_kernel, (core,), (turned, turned_2, proj_grad, proj_grad_2),
-        [shape((depth, half), F32)], project,
-    )
-    back_feats, back_audio = run(
-        back_kernel, (),
-        (audio_1, text_2, weights_21, audio_1_grad, proj_grad_2, text_head),
-        [narrow, square], pair + project, writes=2,
-    )
-    theirs, back_audio, back_feats = tied(theirs, back_audio, back_feats)
+    mine, back_feats, *back_audio = run(
+        back_kernel, (core,),
+        (audio_1, text_2, weights_21, audio_1_grad, text_head, turned, turned_2, proj_grad,
+         proj_grad_2),
+        [shape((depth, half), F32), narrow, shape((rows, half), BF16), shape((rows, half), BF16)],
+        pair + 2 * project, writes=3,
+    )
+    theirs, back_feats, *back_audio = tied(theirs, back_feats, *back_audio)
     plane = lax.axis_size(PLANE)
     part = run(add_kernel, (), (mine, theirs), [shape((plane, depth // plane, half), BF16)], 0)
-    part, back_audio, back_feats = tied(part, back_audio, back_feats)
-    came_audio, came_feats = shifted(back_audio, 1), shifted(back_feats, -2)
+    part, back_feats, *back_audio = tied(part, back_feats, *back_audio)
+    came_feats = shifted(back_feats, -2)
+    came_audio = [shifted(value, 1) for value in back_audio]
     tiles = lax.all_to_all(part, PLANE, 0, 0, tiled=True)
     tile = shared_sum(tiles, lax.axis_size("zl"))
-    came_audio, came_feats, tile = tied(came_audio, came_feats, tile)
+    came_feats, tile, *came_audio = tied(came_feats, tile, *came_audio)
     tiles = lax.all_to_all(tile, "zl", 0, 0, tiled=True)
     tile = shared_sum(tiles, lax.axis_size("zh"))
     came_feats, tile = tied(came_feats, tile)
-    grad_feats, kept = run(
+    grad_audio, grad_feats = run(
         settle_kernel, (),
-        tuple(map(in_hbm, (audio, audio_grad, weights_20, text_2_out, proj_grad_out, text_head,
-                           came_feats))),
-        [narrow, total], pair + project, writes=1,
+        tuple(map(in_hbm, (audio, audio_grad, weights_20, text_2_out, *came_audio, proj_grad_out,
+                           text_head, came_feats))),
+        [square, narrow], pair + project,
     )
     tiles = lax.all_to_all(tile, "zh", 0, 0, tiled=True)
-    tiles, grad_feats, kept = tied(tiles, grad_feats, kept)
+    tiles, grad_audio, grad_feats = tied(tiles, grad_audio, grad_feats)
     spread = shared_sum(tiles, plane)
     spread = lax.all_to_all(spread, PLANE, 0, 0, tiled=True).reshape(depth, half)
-    other_half = other_core(spread)
-    grad_audio = run(finish_kernel, (), (in_hbm(kept), in_hbm(came_audio)), [square], 0)
-    grad_head = run(join_kernel, (core,), (spread, other_half), [shape((depth, wide), BF16)], 0)
+    grad_head = run(
+        join_kernel, (core,), (spread, other_core(spread)), [shape((depth, wide), BF16)], 0
+    )
     return (grad_audio[None], grad_feats[None], grad_head)
 
 

time: 118 us -> 115 us (0.975)
  starting transfers between devices: 45 us -> 52.9 us
  blocking collectives: 26.3 us -> 22.6 us
  waiting for transfers between devices: 22.6 us -> 19.2 us
  Pallas kernels: 21 us -> 17.8 us
    all_to_all x1, waiting for transfers between devices: 9.79 us -> 3.94 us  [body(): tiles = lax.all_to_all(part, PLANE, 0, 0, tiled=True)]
    all_to_all x1, starting transfers between devices: 5.02 us -> 10.7 us  [body(): tiles = lax.all_to_all(tile, 'zh', 0, 0, tiled=True)]
    all_to_all x1, blocking collectives: 18.3 us -> 14.6 us  [body(): lax.all_to_all(spread, PLANE, 0, 0, tiled=True).reshape(depth, half)]
    pallas_call x12 -> x10, Pallas kernels: 21 us -> 17.8 us  [run(): pl.pallas_call(kernel, out_shape=outs[0] if single else outs, in_specs=[s...]
    ppermute x2, starting transfers between devices: 15.6 us -> 17.8 us  [other_core(): return lax.ppermute(value, 'c', [(0, 1), (1, 0)])]
    ppermute x2, waiting for transfers between devices: 0.01 us -> 1.93 us  [other_core(): return lax.ppermute(value, 'c', [(0, 1), (1, 0)])]
    ppermute x4 -> x5, starting transfers between devices: 20.4 us -> 20.2 us  [shifted(): lax.ppermute(value, BLK, [(i, (i + steps) % count) for i in range(count)])]
    ppermute x4 -> x5, waiting for transfers between devices: 4.95 us -> 5.04 us  [shifted(): lax.ppermute(value, BLK, [(i, (i + steps) % count) for i in range(count)])]
  transfers between devices with their start and end apart: 8 -> 9, of which waited for: 3 -> 5; matrix products, arithmetic and copies ran while one was open for 0% -> 0% of each run, Pallas kernels for 13% -> 11%
where the time goes in v4:
time: 115 us
  starting transfers between devices  52.9 us (46%)
  blocking collectives  22.6 us (20%)
  waiting for transfers between devices  19.2 us (17%)
  Pallas kernels  17.8 us (15%)
  between operations  2.11 us (2%)
    ppermute x5, starting transfers between devices, shifted(): lax.ppermute(value, BLK, [(i, (i + steps) % count) for i in range(count)])  20.2 us
    ppermute x2, starting transfers between devices, other_core(): return lax.ppermute(value, 'c', [(0, 1), (1, 0)])  17.8 us
    pallas_call x10, Pallas kernels, run(): pl.pallas_call(kernel, out_shape=outs[0] if single else outs, in_specs=[s...  17.8 us
    all_to_all x1, blocking collectives, body(): lax.all_to_all(spread, PLANE, 0, 0, tiled=True).reshape(depth, half)  14.6 us
    all_to_all x1, starting transfers between devices, body(): tiles = lax.all_to_all(tile, 'zh', 0, 0, tiled=True)  10.7 us
    all_to_all x1, waiting for transfers between devices, body(): tiles = lax.all_to_all(tile, 'zh', 0, 0, tiled=True)  8.25 us
    all_to_all x1, blocking collectives, body(): tiles = lax.all_to_all(tile, 'zl', 0, 0, tiled=True)  8 us
    ppermute x5, waiting for transfers between devices, shifted(): lax.ppermute(value, BLK, [(i, (i + steps) % count) for i in range(count)])  5.04 us
  transfers between devices with their start and end apart: 9, of which 5 were waited for; matrix products, arithmetic and copies ran while one was open for 0% of the time, Pallas kernels for 11%

profile of v4, /device:TPU:1, one launch (start us, length us, event | category | flops | bytes accessed | tf_op | source)
XLA Modules:
  0.0 114.6 jit_solution(17865068719384370594)
XLA Ops:
  0.6 8.8 %collective-permute-start = (bf16[256,1024]{1,0:T(8,128)(2,1)}, bf16[256,1024]{1,0:T(8,128)(2,1)S(1)}, u32[]{:S(2)}, u32[]{:S(2)}) collective-permute-start(bf16[256,1024]{1,0:T(8,128)(2,1)} %bitcast.17), channel_id=1, source_target_pairs={{0,510},{2,0},{4,2},{6,4},{8,6},{10,8},{12,10},{14,12},{16,14},{18... | collective-permute-start | bytes 1572872 | tf_op jit(solution)/shard_map/ppermute | solution.py:16
  9.4 1.9 %collective-permute-start.1 = (bf16[256,768]{1,0:T(8,128)(2,1)}, bf16[256,768]{1,0:T(8,128)(2,1)S(1)}, u32[]{:S(2)}, u32[]{:S(2)}) collective-permute-start(bf16[256,768]{1,0:T(8,128)(2,1)} %bitcast.21), channel_id=1, source_target_pairs={{0,4},{2,6},{4,8},{6,10},{8,12},{10,14},{12,16},{14,18},{16,20},{1... | collective-permute-start | bytes 1179656 | tf_op jit(solution)/shard_map/ppermute | solution.py:16
  12.7 4.2 %shard_map.85 = (bf16[256,1024]{1,0:T(8,128)(2,1)S(1)}, bf16[256,1024]{1,0:T(8,128)(2,1)S(1)}, f32[256,1024]{1,0:T(8,128)S(1)}, f32[256,1]{1,0:T(8,128)S(1)}, f3...) custom-call(f32[1]{0:T(128)} %bitcast.9.scale_ref, f32[1]{0:T(128)} %bitcast.12.bias_ref, ...), custom_call_target="tpu_custom_call" | custom-call | flops 805306368 | bytes 7079936 | tf_op jit(solution)/shard_map/pallas_call | solution.py:203
  16.8 0.0 collective-permute-done.audio_1_ref
  16.9 0.0 copy-start
  16.9 1.9 %shard_map.86 = (bf16[256,1024]{1,0:T(8,128)(2,1)S(1)}, bf16[256,1024]{1,0:T(8,128)(2,1)S(1)}, f32[256,1024]{1,0:T(8,128)S(1)}, bf16[256,1024]{1,0:T(8,128)(2,1)}) custom-call(f32[1]{0:T(128)} %bitcast.10.scale_ref, f32[1]{0:T(128)} %bitcast.13.bias_ref, bf16[256,1024]{1,0:T(8,128)(2,1)S(1)} %collective-permute-done.audio_1_ref, ...), custom_call_target="tpu_custom_call" | custom-call | flops 402653184 | bytes 5768192 | tf_op jit(solution)/shard_map/pallas_call | solution.py:203
  18.8 4.9 %collective-permute-done.1.feats_2_ref = bf16[256,768]{1,0:T(8,128)(2,1)S(1)} collective-permute-done((bf16[256,768]{1,0:T(8,128)(2,1)}, bf16[256,768]{1,0:T(8,128)(2,1)S(1)}, u32[]{:S(2)}, u32[]{:S(2)}) %collective-permute-start.1) | collective-permute-done | bytes 393248 | tf_op jit(solution)/shard_map/ppermute | solution.py:16
  23.8 0.0 copy-done
  23.8 2.3 %shard_map.87 = (bf16[256,1024]{1,0:T(8,128)(2,1)S(1)}, bf16[256,1024]{1,0:T(8,128)(2,1)S(1)}, bf16[768,256]{1,0:T(8,128)(2,1)S(1)}, bf16[768,512]{1,0:T(8,128)(...) custom-call(f32[1]{0:T(128)} %bitcast.11.scale_ref, ...), custom_call_target="tpu_custom_call" | custom-call | flops 1342177280 | bytes 6946816 | tf_op jit(solution)/shard_map/pallas_call | solution.py:203
  26.1 8.4 %collective-permute-start.2 = (bf16[768,512]{1,0:T(8,128)(2,1)S(1)}, bf16[768,512]{1,0:T(8,128)(2,1)S(1)}, u32[]{:S(2)}, u32[]{:S(2)}) collective-permute-start(bf16[768,512]{1,0:T(8,128)(2,1)S(1)} %get-tuple-element.58), channel_id=1, source_target_pairs={{0,2},{2,0},{1,3},{3,1},{4,6},{6,4},{5,7},{7,5},{8,10},{10,8},{9,1... | collective-permute-start | bytes 2359304 | tf_op jit(solution)/shard_map/ppermute | solution.py:20
  34.5 1.8 %shard_map.88 = (f32[768,512]{1,0:T(8,128)S(1)}, bf16[256,768]{1,0:T(8,128)(2,1)}, bf16[256,512]{1,0:T(8,128)(2,1)}, bf16[256,512]{1,0:T(8,128)(2,1)}) custom-call(s32[1]{0:T(128)} %bitcast.core_ref, bf16[256,1024]{1,0:T(8,128)(2,1)S(1)} %collective-permute-done.audio_1_ref, bf16[256,1024]{1,0:T(8,128)(2,1)S(1)} %get-tuple-element.52.text_2_ref, ...), custom_call_target="tpu_custom_call" | custom-call | flops 939524096 | bytes 8126464 | tf_op jit(solution)/shard_map/pallas_call | solution.py:203
  36.4 0.0 collective-permute-done.2.theirs_ref
  36.4 1.0 shard_map.89
  37.5 4.1 %all-to-all-start = ((bf16[16,48,512]{2,1,0:T(8,128)(2,1)}), bf16[16,48,512]{2,1,0:T(8,128)(2,1)S(1)}, u32[]{:S(2)}, u32[]{:S(2)}) async-start(bf16[16,48,512]{2,1,0:T(8,128)(2,1)} %shard_map.89), calls=%async_computation | async-start | bytes 1572864 | tf_op jit(solution)/shard_map/all_to_all | solution.py:267
  41.6 5.6 %collective-permute-start.3 = (bf16[256,768]{1,0:T(8,128)(2,1)S(1)}, bf16[256,768]{1,0:T(8,128)(2,1)S(1)}, u32[]{:S(2)}, u32[]{:S(2)}) collective-permute-start(bf16[256,768]{1,0:T(8,128)(2,1)S(1)} %copy-done.4), channel_id=1, source_target_pairs={{0,508},{2,510},{4,0},{6,2},{8,4},{10,6},{12,8},{14,10},{16,12},{1... | collective-permute-start | bytes 1179656 | tf_op jit(solution)/shard_map/ppermute | solution.py:16
  47.3 1.9 %collective-permute-start.4 = (bf16[256,512]{1,0:T(8,128)(2,1)S(1)}, bf16[256,512]{1,0:T(8,128)(2,1)S(1)}, u32[]{:S(2)}, u32[]{:S(2)}) collective-permute-start(bf16[256,512]{1,0:T(8,128)(2,1)S(1)} %copy-done.6), channel_id=1, source_target_pairs={{0,2},{2,4},{4,6},{6,8},{8,10},{10,12},{12,14},{14,16},{16,18},{18... | collective-permute-start | bytes 786440 | tf_op jit(solution)/shard_map/ppermute | solution.py:16
  49.2 1.9 %collective-permute-start.5 = (bf16[256,512]{1,0:T(8,128)(2,1)S(1)}, bf16[256,512]{1,0:T(8,128)(2,1)S(1)}, u32[]{:S(2)}, u32[]{:S(2)}) collective-permute-start(bf16[256,512]{1,0:T(8,128)(2,1)S(1)} %copy-done.5), channel_id=1, source_target_pairs={{0,2},{2,4},{4,6},{6,8},{8,10},{10,12},{12,14},{14,16},{16,18},{18... | collective-permute-start | bytes 786440 | tf_op jit(solution)/shard_map/ppermute | solution.py:16
  51.1 3.9 %all-to-all-done.tiles_ref = bf16[16,48,512]{2,1,0:T(8,128)(2,1)S(1)} async-done(((bf16[16,48,512]{2,1,0:T(8,128)(2,1)}), bf16[16,48,512]{2,1,0:T(8,128)(2,1)S(1)}, u32[]{:S(2)}, u32[]{:S(2)}) %all-to-all-start) | async-done | bytes 786464 | tf_op jit(solution)/shard_map/all_to_all | solution.py:267
  55.1 0.1 shard_map.90
  55.2 0.0 collective-permute-done.4.came_low_ref
  55.2 0.1 collective-permute-done.5.came_high_ref
  55.3 0.0 collective-permute-done.3.came_feats_ref
  55.3 8.0 %all_to_all.20.tiles_ref = bf16[4,48,512]{2,1,0:T(8,128)(2,1)S(1)} all-to-all(bf16[4,48,512]{2,1,0:T(8,128)(2,1)S(1)} %shard_map.90), channel_id=1, replica_groups=mesh['yl'=2,'x'=4,'zh'=4,'zl'=4,'c'=2,'yh'=2] {'zl'}, dimensions={0} | all-to-all | bytes 393216 | tf_op jit(solution)/shard_map/all_to_all | solution.py:270
  63.3 0.7 shard_map.91
  64.0 10.7 %all-to-all-start.2 = ((bf16[4,48,512]{2,1,0:T(8,128)(2,1)}), bf16[4,48,512]{2,1,0:T(8,128)(2,1)S(1)}, u32[]{:S(2)}, u32[]{:S(2)}) async-start(bf16[4,48,512]{2,1,0:T(8,128)(2,1)} %shard_map.91), calls=%async_computation.2 | async-start | bytes 393216 | tf_op jit(solution)/shard_map/all_to_all | solution.py:279
  74.8 4.3 %shard_map.92 = (bf16[256,1024]{1,0:T(8,128)(2,1)}, bf16[256,768]{1,0:T(8,128)(2,1)}) custom-call(bf16[256,1024]{1,0:T(8,128)(2,1)} %bitcast.19, f32[256,1024]{1,0:T(8,128)} %get-tuple-element.73.grad_ref, bf16[256,256]{1,0:T(8,128)(2,1)} %get-tuple-element.74.weights_20_ref, bf16[256,1024]{1,0:T(8,128)(2,1)} %get-tuple-element.75.text_2_ref, ...), custom_call_target="tpu_custom_call" | custom-call | flops 536870912 | bytes 6160384 | tf_op jit(solution)/shard_map/pallas_call | solution.py:203
  79.1 8.3 %all-to-all-done.2.tiles_ref = bf16[4,48,512]{2,1,0:T(8,128)(2,1)S(1)} async-done(((bf16[4,48,512]{2,1,0:T(8,128)(2,1)}), bf16[4,48,512]{2,1,0:T(8,128)(2,1)S(1)}, u32[]{:S(2)}, u32[]{:S(2)}) %all-to-all-start.2) | async-done | bytes 196640 | tf_op jit(solution)/shard_map/all_to_all | solution.py:279
  87.3 0.1 shard_map.93
  87.4 14.6 %all_to_all.21 = bf16[16,48,512]{2,1,0:T(8,128)(2,1)S(1)} all-to-all(bf16[16,48,512]{2,1,0:T(8,128)(2,1)S(1)} %shard_map.93), channel_id=1, replica_groups=mesh['yl'=2,'x'=4,'zh'=4,'zl'=4,'c'=2,'yh'=2] {'yl','x','yh'}, dimensions={0} | all-to-all | bytes 1572864 | tf_op jit(solution)/shard_map/all_to_all | solution.py:282
  102.0 9.4 %collective-permute-start.6 = (bf16[768,512]{1,0:T(8,128)(2,1)S(1)}, bf16[768,512]{1,0:T(8,128)(2,1)S(1)}, u32[]{:S(2)}, u32[]{:S(2)}) collective-permute-start(bf16[768,512]{1,0:T(8,128)(2,1)S(1)} %bitcast.15), channel_id=1, source_target_pairs={{0,2},{2,0},{1,3},{3,1},{4,6},{6,4},{5,7},{7,5},{8,10},{10,8},{9,1... | collective-permute-start | bytes 2359304 | tf_op jit(solution)/shard_map/ppermute | solution.py:20
  111.5 1.9 %collective-permute-done.6.theirs_ref = bf16[768,512]{1,0:T(8,128)(2,1)S(1)} collective-permute-done((bf16[768,512]{1,0:T(8,128)(2,1)S(1)}, bf16[768,512]{1,0:T(8,128)(2,1)S(1)}, u32[]{:S(2)}, u32[]{:S(2)}) %collective-permute-start.6) | collective-permute-done | bytes 786464 | tf_op jit(solution)/shard_map/ppermute | solution.py:20
  113.3 1.3 %shard_map.94 = bf16[768,1024]{1,0:T(8,128)(2,1)} custom-call(s32[1]{0:T(128)} %bitcast.core_ref, bf16[768,512]{1,0:T(8,128)(2,1)S(1)} %bitcast.16, bf16[768,512]{1,0:T(8,128)(2,1)S(1)} %collective-permute-done.6.theirs_ref), custom_call_target="tpu_custom_call" | custom-call | bytes 3145728 | tf_op jit(solution)/shard_map/pallas_call | solution.py:203
  (12 shorter events, 0.0 us)
Async XLA Ops:
  0.6 16.2 %collective-permute-start = (bf16[256,1024]{1,0:T(8,128)(2,1)}, bf16[256,1024]{1,0:T(8,128)(2,1)S(1)}, u32[]{:S(2)}, u32[]{:S(2)}) collective-permute-start(bf16[256,1024]{1,0:T(8,128)(2,1)} %bitcast.17), channel_id=1, source_target_pairs={{0,510},{2,0},{4,2},{6,4},{8,6},{10,8},{12,10},{14,12},{16,14},{18... | collective-permute-start | bytes 1572872 | tf_op jit(solution)/shard_map/ppermute | solution.py:16
  9.4 14.3 %collective-permute-start.1 = (bf16[256,768]{1,0:T(8,128)(2,1)}, bf16[256,768]{1,0:T(8,128)(2,1)S(1)}, u32[]{:S(2)}, u32[]{:S(2)}) collective-permute-start(bf16[256,768]{1,0:T(8,128)(2,1)} %bitcast.21), channel_id=1, source_target_pairs={{0,4},{2,6},{4,8},{6,10},{8,12},{10,14},{12,16},{14,18},{16,20},{1... | collective-permute-start | bytes 1179656 | tf_op jit(solution)/shard_map/ppermute | solution.py:16
  16.9 6.9 %copy-start = (bf16[768,1024]{1,0:T(8,128)(2,1)S(1)}, bf16[768,1024]{1,0:T(8,128)(2,1)}, u32[]{:S(2)}) copy-start(bf16[768,1024]{1,0:T(8,128)(2,1)} %head_ref.7) | copy-start | bytes 4718596
  26.1 10.3 %collective-permute-start.2 = (bf16[768,512]{1,0:T(8,128)(2,1)S(1)}, bf16[768,512]{1,0:T(8,128)(2,1)S(1)}, u32[]{:S(2)}, u32[]{:S(2)}) collective-permute-start(bf16[768,512]{1,0:T(8,128)(2,1)S(1)} %get-tuple-element.58), channel_id=1, source_target_pairs={{0,2},{2,0},{1,3},{3,1},{4,6},{6,4},{5,7},{7,5},{8,10},{10,8},{9,1... | collective-permute-start | bytes 2359304 | tf_op jit(solution)/shard_map/ppermute | solution.py:20
  37.5 4.2 %copy-start.4 = (bf16[256,768]{1,0:T(8,128)(2,1)S(1)}, bf16[256,768]{1,0:T(8,128)(2,1)}, u32[]{:S(2)}) copy-start(bf16[256,768]{1,0:T(8,128)(2,1)} %get-tuple-element.66) | copy-start | bytes 1179652
  37.5 9.8 %copy-start.6 = (bf16[256,512]{1,0:T(8,128)(2,1)S(1)}, bf16[256,512]{1,0:T(8,128)(2,1)}, u32[]{:S(2)}) copy-start(bf16[256,512]{1,0:T(8,128)(2,1)} %get-tuple-element.68) | copy-start | bytes 786436
  37.5 11.8 %copy-start.5 = (bf16[256,512]{1,0:T(8,128)(2,1)S(1)}, bf16[256,512]{1,0:T(8,128)(2,1)}, u32[]{:S(2)}) copy-start(bf16[256,512]{1,0:T(8,128)(2,1)} %get-tuple-element.69) | copy-start | bytes 786436
  37.5 17.6 %all-to-all-start = ((bf16[16,48,512]{2,1,0:T(8,128)(2,1)}), bf16[16,48,512]{2,1,0:T(8,128)(2,1)S(1)}, u32[]{:S(2)}, u32[]{:S(2)}) async-start(bf16[16,48,512]{2,1,0:T(8,128)(2,1)} %shard_map.89), calls=%async_computation | async-start | bytes 1572864 | tf_op jit(solution)/shard_map/all_to_all | solution.py:267
  41.6 13.7 %collective-permute-start.3 = (bf16[256,768]{1,0:T(8,128)(2,1)S(1)}, bf16[256,768]{1,0:T(8,128)(2,1)S(1)}, u32[]{:S(2)}, u32[]{:S(2)}) collective-permute-start(bf16[256,768]{1,0:T(8,128)(2,1)S(1)} %copy-done.4), channel_id=1, source_target_pairs={{0,508},{2,510},{4,0},{6,2},{8,4},{10,6},{12,8},{14,10},{16,12},{1... | collective-permute-start | bytes 1179656 | tf_op jit(solution)/shard_map/ppermute | solution.py:16
  47.3 7.9 %collective-permute-start.4 = (bf16[256,512]{1,0:T(8,128)(2,1)S(1)}, bf16[256,512]{1,0:T(8,128)(2,1)S(1)}, u32[]{:S(2)}, u32[]{:S(2)}) collective-permute-start(bf16[256,512]{1,0:T(8,128)(2,1)S(1)} %copy-done.6), channel_id=1, source_target_pairs={{0,2},{2,4},{4,6},{6,8},{8,10},{10,12},{12,14},{14,16},{16,18},{18... | collective-permute-start | bytes 786440 | tf_op jit(solution)/shard_map/ppermute | solution.py:16
  49.2 6.1 %collective-permute-start.5 = (bf16[256,512]{1,0:T(8,128)(2,1)S(1)}, bf16[256,512]{1,0:T(8,128)(2,1)S(1)}, u32[]{:S(2)}, u32[]{:S(2)}) collective-permute-start(bf16[256,512]{1,0:T(8,128)(2,1)S(1)} %copy-done.5), channel_id=1, source_target_pairs={{0,2},{2,4},{4,6},{6,8},{8,10},{10,12},{12,14},{14,16},{16,18},{18... | collective-permute-start | bytes 786440 | tf_op jit(solution)/shard_map/ppermute | solution.py:16
  55.2 19.6 %copy-start.2 = (bf16[256,512]{1,0:T(8,128)(2,1)}, bf16[256,512]{1,0:T(8,128)(2,1)S(1)}, u32[]{:S(2)}) copy-start(bf16[256,512]{1,0:T(8,128)(2,1)S(1)} %collective-permute-done.4.came_low_ref) | copy-start | bytes 786436
  55.3 19.5 %copy-start.3 = (bf16[256,512]{1,0:T(8,128)(2,1)}, bf16[256,512]{1,0:T(8,128)(2,1)S(1)}, u32[]{:S(2)}) copy-start(bf16[256,512]{1,0:T(8,128)(2,1)S(1)} %collective-permute-done.5.came_high_ref) | copy-start | bytes 786436
  55.3 19.5 %copy-start.1 = (bf16[256,768]{1,0:T(8,128)(2,1)}, bf16[256,768]{1,0:T(8,128)(2,1)S(1)}, u32[]{:S(2)}) copy-start(bf16[256,768]{1,0:T(8,128)(2,1)S(1)} %collective-permute-done.3.came_feats_ref) | copy-start | bytes 1179652
  64.0 23.3 %all-to-all-start.2 = ((bf16[4,48,512]{2,1,0:T(8,128)(2,1)}), bf16[4,48,512]{2,1,0:T(8,128)(2,1)S(1)}, u32[]{:S(2)}, u32[]{:S(2)}) async-start(bf16[4,48,512]{2,1,0:T(8,128)(2,1)} %shard_map.91), calls=%async_computation.2 | async-start | bytes 393216 | tf_op jit(solution)/shard_map/all_to_all | solution.py:279
  102.0 11.3 %collective-permute-start.6 = (bf16[768,512]{1,0:T(8,128)(2,1)S(1)}, bf16[768,512]{1,0:T(8,128)(2,1)S(1)}, u32[]{:S(2)}, u32[]{:S(2)}) collective-permute-start(bf16[768,512]{1,0:T(8,128)(2,1)S(1)} %bitcast.15), channel_id=1, source_target_pairs={{0,2},{2,0},{1,3},{3,1},{4,6},{6,4},{5,7},{7,5},{8,10},{10,8},{9,1... | collective-permute-start | bytes 2359304 | tf_op jit(solution)/shard_map/ppermute | solution.py:20

commit v5 on v4

--- a/solution.py
+++ b/solution.py
@@ -265,10 +265,10 @@
     came_feats = shifted(back_feats, -2)
     came_audio = [shifted(value, 1) for value in back_audio]
     tiles = lax.all_to_all(part, PLANE, 0, 0, tiled=True)
+    tile = shared_sum(tiles, lax.axis_size("zh"))
+    came_feats, tile, *came_audio = tied(came_feats, tile, *came_audio)
+    tiles = lax.all_to_all(tile, "zh", 0, 0, tiled=True)
     tile = shared_sum(tiles, lax.axis_size("zl"))
-    came_feats, tile, *came_audio = tied(came_feats, tile, *came_audio)
-    tiles = lax.all_to_all(tile, "zl", 0, 0, tiled=True)
-    tile = shared_sum(tiles, lax.axis_size("zh"))
     came_feats, tile = tied(came_feats, tile)
     grad_audio, grad_feats = run(
         settle_kernel, (),
@@ -276,7 +276,7 @@
                            text_head, came_feats))),
         [square, narrow], pair + project,
     )
-    tiles = lax.all_to_all(tile, "zh", 0, 0, tiled=True)
+    tiles = lax.all_to_all(tile, "zl", 0, 0, tiled=True)
     tiles, grad_audio, grad_feats = tied(tiles, grad_audio, grad_feats)
     spread = shared_sum(tiles, plane)
     spread = lax.all_to_all(spread, PLANE, 0, 0, tiled=True).reshape(depth, half)

time: 115 us -> 114 us (level)
  blocking collectives: 22.6 us -> 33.9 us
  waiting for transfers between devices: 19.2 us -> 11.7 us
  starting transfers between devices: 52.9 us -> 47.4 us
    all_to_all x1, blocking collectives: 8 us -> 18.3 us  [body(): tiles = lax.all_to_all(tile, 'zh', 0, 0, tiled=True)]
    all_to_all x1, waiting for transfers between devices: 8.25 us -> 0.79 us  [body(): tiles = lax.all_to_all(tile, 'zl', 0, 0, tiled=True)]
    all_to_all x1, starting transfers between devices: 10.7 us -> 7.44 us  [body(): tiles = lax.all_to_all(tile, 'zl', 0, 0, tiled=True)]
    ppermute x2, starting transfers between devices: 17.8 us -> 15.6 us  [other_core(): return lax.ppermute(value, 'c', [(0, 1), (1, 0)])]
where the time goes in v5:
time: 114 us; the launch traced here: 113 us
  starting transfers between devices  47.4 us (42%)
  blocking collectives  33.9 us (30%)
  Pallas kernels  17.7 us (16%)
  waiting for transfers between devices  11.7 us (10%)
  between operations  2.11 us (2%)
    ppermute x5, starting transfers between devices, shifted(): lax.ppermute(value, BLK, [(i, (i + steps) % count) for i in range(count)])  20.2 us
    all_to_all x1, blocking collectives, body(): tiles = lax.all_to_all(tile, 'zh', 0, 0, tiled=True)  18.3 us
    pallas_call x10, Pallas kernels, run(): pl.pallas_call(kernel, out_shape=outs[0] if single else outs, in_specs=[s...  17.7 us
    ppermute x2, starting transfers between devices, other_core(): return lax.ppermute(value, 'c', [(0, 1), (1, 0)])  15.6 us
    all_to_all x1, blocking collectives, body(): lax.all_to_all(spread, PLANE, 0, 0, tiled=True).reshape(depth, half)  15.6 us
    all_to_all x1, starting transfers between devices, body(): tiles = lax.all_to_all(tile, 'zl', 0, 0, tiled=True)  7.44 us
    ppermute x5, waiting for transfers between devices, shifted(): lax.ppermute(value, BLK, [(i, (i + steps) % count) for i in range(count)])  5.04 us
    all_to_all x1, starting transfers between devices, body(): tiles = lax.all_to_all(part, PLANE, 0, 0, tiled=True)  4.14 us
  transfers between devices with their start and end apart: 9, of which 5 were waited for; matrix products, arithmetic and copies ran while one was open for 0% of the time, Pallas kernels for 11%

profile of v5, /device:TPU:1, one launch (start us, length us, event | category | flops | bytes accessed | tf_op | source)
XLA Modules:
  0.0 112.9 jit_solution(4136436669359898655)
XLA Ops:
  0.6 8.8 %collective-permute-start = (bf16[256,1024]{1,0:T(8,128)(2,1)}, bf16[256,1024]{1,0:T(8,128)(2,1)S(1)}, u32[]{:S(2)}, u32[]{:S(2)}) collective-permute-start(bf16[256,1024]{1,0:T(8,128)(2,1)} %bitcast.17), channel_id=1, source_target_pairs={{0,510},{2,0},{4,2},{6,4},{8,6},{10,8},{12,10},{14,12},{16,14},{18... | collective-permute-start | bytes 1572872 | tf_op jit(solution)/shard_map/ppermute | solution.py:16
  9.4 1.9 %collective-permute-start.1 = (bf16[256,768]{1,0:T(8,128)(2,1)}, bf16[256,768]{1,0:T(8,128)(2,1)S(1)}, u32[]{:S(2)}, u32[]{:S(2)}) collective-permute-start(bf16[256,768]{1,0:T(8,128)(2,1)} %bitcast.21), channel_id=1, source_target_pairs={{0,4},{2,6},{4,8},{6,10},{8,12},{10,14},{12,16},{14,18},{16,20},{1... | collective-permute-start | bytes 1179656 | tf_op jit(solution)/shard_map/ppermute | solution.py:16
  12.7 4.2 %shard_map.85 = (bf16[256,1024]{1,0:T(8,128)(2,1)S(1)}, bf16[256,1024]{1,0:T(8,128)(2,1)S(1)}, f32[256,1024]{1,0:T(8,128)S(1)}, f32[256,1]{1,0:T(8,128)S(1)}, f3...) custom-call(f32[1]{0:T(128)} %bitcast.9.scale_ref, f32[1]{0:T(128)} %bitcast.12.bias_ref, ...), custom_call_target="tpu_custom_call" | custom-call | flops 805306368 | bytes 7079936 | tf_op jit(solution)/shard_map/pallas_call | solution.py:203
  16.8 0.0 collective-permute-done.audio_1_ref
  16.9 0.0 copy-start
  16.9 1.9 %shard_map.86 = (bf16[256,1024]{1,0:T(8,128)(2,1)S(1)}, bf16[256,1024]{1,0:T(8,128)(2,1)S(1)}, f32[256,1024]{1,0:T(8,128)S(1)}, bf16[256,1024]{1,0:T(8,128)(2,1)}) custom-call(f32[1]{0:T(128)} %bitcast.10.scale_ref, f32[1]{0:T(128)} %bitcast.13.bias_ref, bf16[256,1024]{1,0:T(8,128)(2,1)S(1)} %collective-permute-done.audio_1_ref, ...), custom_call_target="tpu_custom_call" | custom-call | flops 402653184 | bytes 5768192 | tf_op jit(solution)/shard_map/pallas_call | solution.py:203
  18.8 4.9 %collective-permute-done.1.feats_2_ref = bf16[256,768]{1,0:T(8,128)(2,1)S(1)} collective-permute-done((bf16[256,768]{1,0:T(8,128)(2,1)}, bf16[256,768]{1,0:T(8,128)(2,1)S(1)}, u32[]{:S(2)}, u32[]{:S(2)}) %collective-permute-start.1) | collective-permute-done | bytes 393248 | tf_op jit(solution)/shard_map/ppermute | solution.py:16
  23.8 2.3 %shard_map.87 = (bf16[256,1024]{1,0:T(8,128)(2,1)S(1)}, bf16[256,1024]{1,0:T(8,128)(2,1)S(1)}, bf16[768,256]{1,0:T(8,128)(2,1)S(1)}, bf16[768,512]{1,0:T(8,128)(...) custom-call(f32[1]{0:T(128)} %bitcast.11.scale_ref, ...), custom_call_target="tpu_custom_call" | custom-call | flops 1342177280 | bytes 6946816 | tf_op jit(solution)/shard_map/pallas_call | solution.py:203
  26.1 8.4 %collective-permute-start.2 = (bf16[768,512]{1,0:T(8,128)(2,1)S(1)}, bf16[768,512]{1,0:T(8,128)(2,1)S(1)}, u32[]{:S(2)}, u32[]{:S(2)}) collective-permute-start(bf16[768,512]{1,0:T(8,128)(2,1)S(1)} %get-tuple-element.58), channel_id=1, source_target_pairs={{0,2},{2,0},{1,3},{3,1},{4,6},{6,4},{5,7},{7,5},{8,10},{10,8},{9,1... | collective-permute-start | bytes 2359304 | tf_op jit(solution)/shard_map/ppermute | solution.py:20
  34.5 1.8 %shard_map.88 = (f32[768,512]{1,0:T(8,128)S(1)}, bf16[256,768]{1,0:T(8,128)(2,1)}, bf16[256,512]{1,0:T(8,128)(2,1)}, bf16[256,512]{1,0:T(8,128)(2,1)}) custom-call(s32[1]{0:T(128)} %bitcast.core_ref, bf16[256,1024]{1,0:T(8,128)(2,1)S(1)} %collective-permute-done.audio_1_ref, bf16[256,1024]{1,0:T(8,128)(2,1)S(1)} %get-tuple-element.52.text_2_ref, ...), custom_call_target="tpu_custom_call" | custom-call | flops 939524096 | bytes 8126464 | tf_op jit(solution)/shard_map/pallas_call | solution.py:203
  36.4 0.0 collective-permute-done.2.theirs_ref
  36.4 1.0 shard_map.89
  37.5 4.1 %all-to-all-start = ((bf16[16,48,512]{2,1,0:T(8,128)(2,1)}), bf16[16,48,512]{2,1,0:T(8,128)(2,1)S(1)}, u32[]{:S(2)}, u32[]{:S(2)}) async-start(bf16[16,48,512]{2,1,0:T(8,128)(2,1)} %shard_map.89), calls=%async_computation | async-start | bytes 1572864 | tf_op jit(solution)/shard_map/all_to_all | solution.py:267
  41.6 5.6 %collective-permute-start.3 = (bf16[256,768]{1,0:T(8,128)(2,1)S(1)}, bf16[256,768]{1,0:T(8,128)(2,1)S(1)}, u32[]{:S(2)}, u32[]{:S(2)}) collective-permute-start(bf16[256,768]{1,0:T(8,128)(2,1)S(1)} %copy-done.4), channel_id=1, source_target_pairs={{0,508},{2,510},{4,0},{6,2},{8,4},{10,6},{12,8},{14,10},{16,12},{1... | collective-permute-start | bytes 1179656 | tf_op jit(solution)/shard_map/ppermute | solution.py:16
  47.3 1.9 %collective-permute-start.4 = (bf16[256,512]{1,0:T(8,128)(2,1)S(1)}, bf16[256,512]{1,0:T(8,128)(2,1)S(1)}, u32[]{:S(2)}, u32[]{:S(2)}) collective-permute-start(bf16[256,512]{1,0:T(8,128)(2,1)S(1)} %copy-done.6), channel_id=1, source_target_pairs={{0,2},{2,4},{4,6},{6,8},{8,10},{10,12},{12,14},{14,16},{16,18},{18... | collective-permute-start | bytes 786440 | tf_op jit(solution)/shard_map/ppermute | solution.py:16
  49.2 1.9 %collective-permute-start.5 = (bf16[256,512]{1,0:T(8,128)(2,1)S(1)}, bf16[256,512]{1,0:T(8,128)(2,1)S(1)}, u32[]{:S(2)}, u32[]{:S(2)}) collective-permute-start(bf16[256,512]{1,0:T(8,128)(2,1)S(1)} %copy-done.5), channel_id=1, source_target_pairs={{0,2},{2,4},{4,6},{6,8},{8,10},{10,12},{12,14},{14,16},{16,18},{18... | collective-permute-start | bytes 786440 | tf_op jit(solution)/shard_map/ppermute | solution.py:16
  51.1 3.9 %all-to-all-done.tiles_ref = bf16[16,48,512]{2,1,0:T(8,128)(2,1)S(1)} async-done(((bf16[16,48,512]{2,1,0:T(8,128)(2,1)}), bf16[16,48,512]{2,1,0:T(8,128)(2,1)S(1)}, u32[]{:S(2)}, u32[]{:S(2)}) %all-to-all-start) | async-done | bytes 786464 | tf_op jit(solution)/shard_map/all_to_all | solution.py:267
  55.1 0.1 shard_map.90
  55.2 0.0 collective-permute-done.4.came_low_ref
  55.2 0.1 collective-permute-done.5.came_high_ref
  55.3 0.0 collective-permute-done.3.came_feats_ref
  55.3 18.3 %all_to_all.20.tiles_ref = bf16[4,48,512]{2,1,0:T(8,128)(2,1)S(1)} all-to-all(bf16[4,48,512]{2,1,0:T(8,128)(2,1)S(1)} %shard_map.90), channel_id=1, replica_groups=mesh['yl'=2,'x'=4,'zh'=4,'zl'=4,'c'=2,'yh'=2] {'zh'}, dimensions={0} | all-to-all | bytes 393216 | tf_op jit(solution)/shard_map/all_to_all | solution.py:270
  73.6 0.7 shard_map.91
  74.3 7.4 %all-to-all-start.2 = ((bf16[4,48,512]{2,1,0:T(8,128)(2,1)}), bf16[4,48,512]{2,1,0:T(8,128)(2,1)S(1)}, u32[]{:S(2)}, u32[]{:S(2)}) async-start(bf16[4,48,512]{2,1,0:T(8,128)(2,1)} %shard_map.91), calls=%async_computation.2 | async-start | bytes 393216 | tf_op jit(solution)/shard_map/all_to_all | solution.py:279
  81.8 0.0 copy-done.1
  81.8 4.3 %shard_map.92 = (bf16[256,1024]{1,0:T(8,128)(2,1)}, bf16[256,768]{1,0:T(8,128)(2,1)}) custom-call(bf16[256,1024]{1,0:T(8,128)(2,1)} %bitcast.19, f32[256,1024]{1,0:T(8,128)} %get-tuple-element.73.grad_ref, bf16[256,256]{1,0:T(8,128)(2,1)} %get-tuple-element.74.weights_20_ref, bf16[256,1024]{1,0:T(8,128)(2,1)} %get-tuple-element.75.text_2_ref, ...), custom_call_target="tpu_custom_call" | custom-call | flops 536870912 | bytes 6160384 | tf_op jit(solution)/shard_map/pallas_call | solution.py:203
  86.1 0.8 all-to-all-done.2.tiles_ref
  86.9 0.1 shard_map.93
  86.9 15.6 %all_to_all.21 = bf16[16,48,512]{2,1,0:T(8,128)(2,1)S(1)} all-to-all(bf16[16,48,512]{2,1,0:T(8,128)(2,1)S(1)} %shard_map.93), channel_id=1, replica_groups=mesh['yl'=2,'x'=4,'zh'=4,'zl'=4,'c'=2,'yh'=2] {'yl','x','yh'}, dimensions={0} | all-to-all | bytes 1572864 | tf_op jit(solution)/shard_map/all_to_all | solution.py:282
  102.6 7.2 %collective-permute-start.6 = (bf16[768,512]{1,0:T(8,128)(2,1)S(1)}, bf16[768,512]{1,0:T(8,128)(2,1)S(1)}, u32[]{:S(2)}, u32[]{:S(2)}) collective-permute-start(bf16[768,512]{1,0:T(8,128)(2,1)S(1)} %bitcast.15), channel_id=1, source_target_pairs={{0,2},{2,0},{1,3},{3,1},{4,6},{6,4},{5,7},{7,5},{8,10},{10,8},{9,1... | collective-permute-start | bytes 2359304 | tf_op jit(solution)/shard_map/ppermute | solution.py:20
  109.8 1.9 %collective-permute-done.6.theirs_ref = bf16[768,512]{1,0:T(8,128)(2,1)S(1)} collective-permute-done((bf16[768,512]{1,0:T(8,128)(2,1)S(1)}, bf16[768,512]{1,0:T(8,128)(2,1)S(1)}, u32[]{:S(2)}, u32[]{:S(2)}) %collective-permute-start.6) | collective-permute-done | bytes 786464 | tf_op jit(solution)/shard_map/ppermute | solution.py:20
  111.7 1.3 %shard_map.94 = bf16[768,1024]{1,0:T(8,128)(2,1)} custom-call(s32[1]{0:T(128)} %bitcast.core_ref, bf16[768,512]{1,0:T(8,128)(2,1)S(1)} %bitcast.16, bf16[768,512]{1,0:T(8,128)(2,1)S(1)} %collective-permute-done.6.theirs_ref), custom_call_target="tpu_custom_call" | custom-call | bytes 3145728 | tf_op jit(solution)/shard_map/pallas_call | solution.py:203
  (12 shorter events, 0.0 us)
Async XLA Ops:
  0.6 16.2 %collective-permute-start = (bf16[256,1024]{1,0:T(8,128)(2,1)}, bf16[256,1024]{1,0:T(8,128)(2,1)S(1)}, u32[]{:S(2)}, u32[]{:S(2)}) collective-permute-start(bf16[256,1024]{1,0:T(8,128)(2,1)} %bitcast.17), channel_id=1, source_target_pairs={{0,510},{2,0},{4,2},{6,4},{8,6},{10,8},{12,10},{14,12},{16,14},{18... | collective-permute-start | bytes 1572872 | tf_op jit(solution)/shard_map/ppermute | solution.py:16
  9.4 14.3 %collective-permute-start.1 = (bf16[256,768]{1,0:T(8,128)(2,1)}, bf16[256,768]{1,0:T(8,128)(2,1)S(1)}, u32[]{:S(2)}, u32[]{:S(2)}) collective-permute-start(bf16[256,768]{1,0:T(8,128)(2,1)} %bitcast.21), channel_id=1, source_target_pairs={{0,4},{2,6},{4,8},{6,10},{8,12},{10,14},{12,16},{14,18},{16,20},{1... | collective-permute-start | bytes 1179656 | tf_op jit(solution)/shard_map/ppermute | solution.py:16
  16.9 6.9 %copy-start = (bf16[768,1024]{1,0:T(8,128)(2,1)S(1)}, bf16[768,1024]{1,0:T(8,128)(2,1)}, u32[]{:S(2)}) copy-start(bf16[768,1024]{1,0:T(8,128)(2,1)} %head_ref.7) | copy-start | bytes 4718596
  26.1 10.3 %collective-permute-start.2 = (bf16[768,512]{1,0:T(8,128)(2,1)S(1)}, bf16[768,512]{1,0:T(8,128)(2,1)S(1)}, u32[]{:S(2)}, u32[]{:S(2)}) collective-permute-start(bf16[768,512]{1,0:T(8,128)(2,1)S(1)} %get-tuple-element.58), channel_id=1, source_target_pairs={{0,2},{2,0},{1,3},{3,1},{4,6},{6,4},{5,7},{7,5},{8,10},{10,8},{9,1... | collective-permute-start | bytes 2359304 | tf_op jit(solution)/shard_map/ppermute | solution.py:20
  37.5 4.2 %copy-start.4 = (bf16[256,768]{1,0:T(8,128)(2,1)S(1)}, bf16[256,768]{1,0:T(8,128)(2,1)}, u32[]{:S(2)}) copy-start(bf16[256,768]{1,0:T(8,128)(2,1)} %get-tuple-element.66) | copy-start | bytes 1179652
  37.5 9.8 %copy-start.6 = (bf16[256,512]{1,0:T(8,128)(2,1)S(1)}, bf16[256,512]{1,0:T(8,128)(2,1)}, u32[]{:S(2)}) copy-start(bf16[256,512]{1,0:T(8,128)(2,1)} %get-tuple-element.68) | copy-start | bytes 786436
  37.5 11.8 %copy-start.5 = (bf16[256,512]{1,0:T(8,128)(2,1)S(1)}, bf16[256,512]{1,0:T(8,128)(2,1)}, u32[]{:S(2)}) copy-start(bf16[256,512]{1,0:T(8,128)(2,1)} %get-tuple-element.69) | copy-start | bytes 786436
  37.5 17.6 %all-to-all-start = ((bf16[16,48,512]{2,1,0:T(8,128)(2,1)}), bf16[16,48,512]{2,1,0:T(8,128)(2,1)S(1)}, u32[]{:S(2)}, u32[]{:S(2)}) async-start(bf16[16,48,512]{2,1,0:T(8,128)(2,1)} %shard_map.89), calls=%async_computation | async-start | bytes 1572864 | tf_op jit(solution)/shard_map/all_to_all | solution.py:267
  41.6 13.7 %collective-permute-start.3 = (bf16[256,768]{1,0:T(8,128)(2,1)S(1)}, bf16[256,768]{1,0:T(8,128)(2,1)S(1)}, u32[]{:S(2)}, u32[]{:S(2)}) collective-permute-start(bf16[256,768]{1,0:T(8,128)(2,1)S(1)} %copy-done.4), channel_id=1, source_target_pairs={{0,508},{2,510},{4,0},{6,2},{8,4},{10,6},{12,8},{14,10},{16,12},{1... | collective-permute-start | bytes 1179656 | tf_op jit(solution)/shard_map/ppermute | solution.py:16
  47.3 7.9 %collective-permute-start.4 = (bf16[256,512]{1,0:T(8,128)(2,1)S(1)}, bf16[256,512]{1,0:T(8,128)(2,1)S(1)}, u32[]{:S(2)}, u32[]{:S(2)}) collective-permute-start(bf16[256,512]{1,0:T(8,128)(2,1)S(1)} %copy-done.6), channel_id=1, source_target_pairs={{0,2},{2,4},{4,6},{6,8},{8,10},{10,12},{12,14},{14,16},{16,18},{18... | collective-permute-start | bytes 786440 | tf_op jit(solution)/shard_map/ppermute | solution.py:16
  49.2 6.1 %collective-permute-start.5 = (bf16[256,512]{1,0:T(8,128)(2,1)S(1)}, bf16[256,512]{1,0:T(8,128)(2,1)S(1)}, u32[]{:S(2)}, u32[]{:S(2)}) collective-permute-start(bf16[256,512]{1,0:T(8,128)(2,1)S(1)} %copy-done.5), channel_id=1, source_target_pairs={{0,2},{2,4},{4,6},{6,8},{8,10},{10,12},{12,14},{14,16},{16,18},{18... | collective-permute-start | bytes 786440 | tf_op jit(solution)/shard_map/ppermute | solution.py:16
  55.2 26.6 %copy-start.2 = (bf16[256,512]{1,0:T(8,128)(2,1)}, bf16[256,512]{1,0:T(8,128)(2,1)S(1)}, u32[]{:S(2)}) copy-start(bf16[256,512]{1,0:T(8,128)(2,1)S(1)} %collective-permute-done.4.came_low_ref) | copy-start | bytes 786436
  55.3 26.4 %copy-start.3 = (bf16[256,512]{1,0:T(8,128)(2,1)}, bf16[256,512]{1,0:T(8,128)(2,1)S(1)}, u32[]{:S(2)}) copy-start(bf16[256,512]{1,0:T(8,128)(2,1)S(1)} %collective-permute-done.5.came_high_ref) | copy-start | bytes 786436
  55.3 26.4 %copy-start.1 = (bf16[256,768]{1,0:T(8,128)(2,1)}, bf16[256,768]{1,0:T(8,128)(2,1)S(1)}, u32[]{:S(2)}) copy-start(bf16[256,768]{1,0:T(8,128)(2,1)S(1)} %collective-permute-done.3.came_feats_ref) | copy-start | bytes 1179652
  74.3 12.5 %all-to-all-start.2 = ((bf16[4,48,512]{2,1,0:T(8,128)(2,1)}), bf16[4,48,512]{2,1,0:T(8,128)(2,1)S(1)}, u32[]{:S(2)}, u32[]{:S(2)}) async-start(bf16[4,48,512]{2,1,0:T(8,128)(2,1)} %shard_map.91), calls=%async_computation.2 | async-start | bytes 393216 | tf_op jit(solution)/shard_map/all_to_all | solution.py:279
  102.6 9.1 %collective-permute-start.6 = (bf16[768,512]{1,0:T(8,128)(2,1)S(1)}, bf16[768,512]{1,0:T(8,128)(2,1)S(1)}, u32[]{:S(2)}, u32[]{:S(2)}) collective-permute-start(bf16[768,512]{1,0:T(8,128)(2,1)S(1)} %bitcast.15), channel_id=1, source_target_pairs={{0,2},{2,0},{1,3},{3,1},{4,6},{6,4},{5,7},{7,5},{8,10},{10,8},{9,1... | collective-permute-start | bytes 2359304 | tf_op jit(solution)/shard_map/ppermute | solution.py:20

commit v6 on v5

--- a/solution.py
+++ b/solution.py
@@ -126,9 +126,18 @@
     second.wait()
 
 
-def add_kernel(mine_ref, theirs_ref, out_ref):
-    total = mine_ref[...] + theirs_ref[...].astype(F32)
-    out_ref[...] = total.astype(BF16).reshape(out_ref.shape)
+def add_kernel(mine_ref, theirs_ref, out_hbm, out_ref, left):
+    tiles, depth, width = out_ref.shape
+    chunk, copies = tiles // 4, []
+    for i in range(4):
+        rows = slice(i * chunk * depth, (i + 1) * chunk * depth)
+        total = mine_ref[rows, :] + theirs_ref[rows, :].astype(F32)
+        out_ref[i * chunk : (i + 1) * chunk] = total.astype(BF16).reshape(chunk, depth, width)
+        part = pl.ds(i * chunk, chunk)
+        copies.append(pltpu.make_async_copy(out_ref.at[part], out_hbm.at[part], left.at[i]))
+        copies[-1].start()
+    for copy in copies:
+        copy.wait()
 
 
 def back_kernel(
@@ -198,7 +207,7 @@
     kept = len(outs) - writes
     scratch = [pltpu.VMEM(a.shape, a.dtype) for a in outs[kept:]]
     if writes:
-        scratch.append(pltpu.SemaphoreType.DMA((writes,)))
+        scratch.append(pltpu.SemaphoreType.DMA((max(writes, 4),)))
     outs = outs[:kept] + [pltpu.HBM(a.shape, a.dtype) for a in outs[kept:]]
     return pl.pallas_call(
         kernel,
@@ -260,7 +269,9 @@
     )
     theirs, back_feats, *back_audio = tied(theirs, back_feats, *back_audio)
     plane = lax.axis_size(PLANE)
-    part = run(add_kernel, (), (mine, theirs), [shape((plane, depth // plane, half), BF16)], 0)
+    part = run(
+        add_kernel, (), (mine, theirs), [shape((plane, depth // plane, half), BF16)], 0, writes=1
+    )
     part, back_feats, *back_audio = tied(part, back_feats, *back_audio)
     came_feats = shifted(back_feats, -2)
     came_audio = [shifted(value, 1) for value in back_audio]

time: 114 us -> 115 us (level)
  Pallas kernels: 17.7 us -> 18.9 us
  transfers between devices with their start and end apart: 9 -> 9, of which waited for: 5 -> 6; matrix products, arithmetic and copies ran while one was open for 0% -> 0% of each run, Pallas kernels for 11% -> 11%
where the time goes in v6:
time: 115 us; the launch traced here: 114 us
  starting transfers between devices  47.6 us (41%)
  blocking collectives  33.8 us (29%)
  Pallas kernels  18.9 us (16%)
  waiting for transfers between devices  11.7 us (10%)
  between operations  2.14 us (2%)
    ppermute x5, starting transfers between devices, shifted(): lax.ppermute(value, BLK, [(i, (i + steps) % count) for i in range(count)])  20.3 us
    pallas_call x10, Pallas kernels, run(): pl.pallas_call(kernel, out_shape=outs[0] if single else outs, in_specs=[s...  18.9 us
    all_to_all x1, blocking collectives, body(): tiles = lax.all_to_all(tile, 'zh', 0, 0, tiled=True)  18.3 us
    ppermute x2, starting transfers between devices, other_core(): return lax.ppermute(value, 'c', [(0, 1), (1, 0)])  15.6 us
    all_to_all x1, blocking collectives, body(): lax.all_to_all(spread, PLANE, 0, 0, tiled=True).reshape(depth, half)  15.5 us
    all_to_all x1, starting transfers between devices, body(): tiles = lax.all_to_all(tile, 'zl', 0, 0, tiled=True)  7.55 us
    ppermute x5, waiting for transfers between devices, shifted(): lax.ppermute(value, BLK, [(i, (i + steps) % count) for i in range(count)])  5.05 us
    all_to_all x1, starting transfers between devices, body(): tiles = lax.all_to_all(part, PLANE, 0, 0, tiled=True)  4.14 us
  transfers between devices with their start and end apart: 9, of which 6 were waited for; matrix products, arithmetic and copies ran while one was open for 0% of the time, Pallas kernels for 11%

profile of v6, /device:TPU:1, one launch (start us, length us, event | category | flops | bytes accessed | tf_op | source)
XLA Modules:
  0.0 114.1 jit_solution(15246140745960118097)
XLA Ops:
  0.6 8.8 %collective-permute-start = (bf16[256,1024]{1,0:T(8,128)(2,1)}, bf16[256,1024]{1,0:T(8,128)(2,1)S(1)}, u32[]{:S(2)}, u32[]{:S(2)}) collective-permute-start(bf16[256,1024]{1,0:T(8,128)(2,1)} %bitcast.17), channel_id=1, source_target_pairs={{0,510},{2,0},{4,2},{6,4},{8,6},{10,8},{12,10},{14,12},{16,14},{18... | collective-permute-start | bytes 1572872 | tf_op jit(solution)/shard_map/ppermute | solution.py:16
  9.4 1.9 %collective-permute-start.1 = (bf16[256,768]{1,0:T(8,128)(2,1)}, bf16[256,768]{1,0:T(8,128)(2,1)S(1)}, u32[]{:S(2)}, u32[]{:S(2)}) collective-permute-start(bf16[256,768]{1,0:T(8,128)(2,1)} %bitcast.21), channel_id=1, source_target_pairs={{0,4},{2,6},{4,8},{6,10},{8,12},{10,14},{12,16},{14,18},{16,20},{1... | collective-permute-start | bytes 1179656 | tf_op jit(solution)/shard_map/ppermute | solution.py:16
  12.7 4.2 %shard_map.85 = (bf16[256,1024]{1,0:T(8,128)(2,1)S(1)}, bf16[256,1024]{1,0:T(8,128)(2,1)S(1)}, f32[256,1024]{1,0:T(8,128)S(1)}, f32[256,1]{1,0:T(8,128)S(1)}, f3...) custom-call(f32[1]{0:T(128)} %bitcast.9.scale_ref, f32[1]{0:T(128)} %bitcast.12.bias_ref, ...), custom_call_target="tpu_custom_call" | custom-call | flops 805306368 | bytes 7079936 | tf_op jit(solution)/shard_map/pallas_call | solution.py:212
  16.9 0.0 collective-permute-done.audio_1_ref
  16.9 0.0 copy-start
  16.9 2.0 %shard_map.86 = (bf16[256,1024]{1,0:T(8,128)(2,1)S(1)}, bf16[256,1024]{1,0:T(8,128)(2,1)S(1)}, f32[256,1024]{1,0:T(8,128)S(1)}, bf16[256,1024]{1,0:T(8,128)(2,1)}) custom-call(f32[1]{0:T(128)} %bitcast.10.scale_ref, f32[1]{0:T(128)} %bitcast.13.bias_ref, bf16[256,1024]{1,0:T(8,128)(2,1)S(1)} %collective-permute-done.audio_1_ref, ...), custom_call_target="tpu_custom_call" | custom-call | flops 402653184 | bytes 5768192 | tf_op jit(solution)/shard_map/pallas_call | solution.py:212
  18.9 4.9 %collective-permute-done.1.feats_2_ref = bf16[256,768]{1,0:T(8,128)(2,1)S(1)} collective-permute-done((bf16[256,768]{1,0:T(8,128)(2,1)}, bf16[256,768]{1,0:T(8,128)(2,1)S(1)}, u32[]{:S(2)}, u32[]{:S(2)}) %collective-permute-start.1) | collective-permute-done | bytes 393248 | tf_op jit(solution)/shard_map/ppermute | solution.py:16
  23.8 2.4 %shard_map.87 = (bf16[256,1024]{1,0:T(8,128)(2,1)S(1)}, bf16[256,1024]{1,0:T(8,128)(2,1)S(1)}, bf16[768,256]{1,0:T(8,128)(2,1)S(1)}, bf16[768,512]{1,0:T(8,128)(...) custom-call(f32[1]{0:T(128)} %bitcast.11.scale_ref, ...), custom_call_target="tpu_custom_call" | custom-call | flops 1342177280 | bytes 6946816 | tf_op jit(solution)/shard_map/pallas_call | solution.py:212
  26.1 8.4 %collective-permute-start.2 = (bf16[768,512]{1,0:T(8,128)(2,1)S(1)}, bf16[768,512]{1,0:T(8,128)(2,1)S(1)}, u32[]{:S(2)}, u32[]{:S(2)}) collective-permute-start(bf16[768,512]{1,0:T(8,128)(2,1)S(1)} %get-tuple-element.58), channel_id=1, source_target_pairs={{0,2},{2,0},{1,3},{3,1},{4,6},{6,4},{5,7},{7,5},{8,10},{10,8},{9,1... | collective-permute-start | bytes 2359304 | tf_op jit(solution)/shard_map/ppermute | solution.py:20
  34.6 1.8 %shard_map.88 = (f32[768,512]{1,0:T(8,128)S(1)}, bf16[256,768]{1,0:T(8,128)(2,1)}, bf16[256,512]{1,0:T(8,128)(2,1)}, bf16[256,512]{1,0:T(8,128)(2,1)}) custom-call(s32[1]{0:T(128)} %bitcast.core_ref, bf16[256,1024]{1,0:T(8,128)(2,1)S(1)} %collective-permute-done.audio_1_ref, bf16[256,1024]{1,0:T(8,128)(2,1)S(1)} %get-tuple-element.52.text_2_ref, ...), custom_call_target="tpu_custom_call" | custom-call | flops 939524096 | bytes 8126464 | tf_op jit(solution)/shard_map/pallas_call | solution.py:212
  36.4 0.1 collective-permute-done.2.theirs_ref
  36.5 2.1 %shard_map.89 = bf16[16,48,512]{2,1,0:T(8,128)(2,1)} custom-call(f32[768,512]{1,0:T(8,128)S(1)} %get-tuple-element.57.mine_ref, bf16[768,512]{1,0:T(8,128)(2,1)S(1)} %collective-permute-done.2.theirs_ref), custom_call_target="tpu_custom_call" | custom-call | bytes 3145728 | tf_op jit(solution)/shard_map/pallas_call | solution.py:212
  38.5 0.0 copy-start.4
  38.6 0.0 copy-start.6
  38.6 4.1 %all-to-all-start = ((bf16[16,48,512]{2,1,0:T(8,128)(2,1)}), bf16[16,48,512]{2,1,0:T(8,128)(2,1)S(1)}, u32[]{:S(2)}, u32[]{:S(2)}) async-start(bf16[16,48,512]{2,1,0:T(8,128)(2,1)} %shard_map.89), calls=%async_computation | async-start | bytes 1572864 | tf_op jit(solution)/shard_map/all_to_all | solution.py:278
  42.7 5.7 %collective-permute-start.3 = (bf16[256,768]{1,0:T(8,128)(2,1)S(1)}, bf16[256,768]{1,0:T(8,128)(2,1)S(1)}, u32[]{:S(2)}, u32[]{:S(2)}) collective-permute-start(bf16[256,768]{1,0:T(8,128)(2,1)S(1)} %copy-done.4), channel_id=1, source_target_pairs={{0,508},{2,510},{4,0},{6,2},{8,4},{10,6},{12,8},{14,10},{16,12},{1... | collective-permute-start | bytes 1179656 | tf_op jit(solution)/shard_map/ppermute | solution.py:16
  48.5 1.9 %collective-permute-start.4 = (bf16[256,512]{1,0:T(8,128)(2,1)S(1)}, bf16[256,512]{1,0:T(8,128)(2,1)S(1)}, u32[]{:S(2)}, u32[]{:S(2)}) collective-permute-start(bf16[256,512]{1,0:T(8,128)(2,1)S(1)} %copy-done.6), channel_id=1, source_target_pairs={{0,2},{2,4},{4,6},{6,8},{8,10},{10,12},{12,14},{14,16},{16,18},{18... | collective-permute-start | bytes 786440 | tf_op jit(solution)/shard_map/ppermute | solution.py:16
  50.4 1.9 %collective-permute-start.5 = (bf16[256,512]{1,0:T(8,128)(2,1)S(1)}, bf16[256,512]{1,0:T(8,128)(2,1)S(1)}, u32[]{:S(2)}, u32[]{:S(2)}) collective-permute-start(bf16[256,512]{1,0:T(8,128)(2,1)S(1)} %copy-done.5), channel_id=1, source_target_pairs={{0,2},{2,4},{4,6},{6,8},{8,10},{10,12},{12,14},{14,16},{16,18},{18... | collective-permute-start | bytes 786440 | tf_op jit(solution)/shard_map/ppermute | solution.py:16
  52.3 3.9 %all-to-all-done.tiles_ref = bf16[16,48,512]{2,1,0:T(8,128)(2,1)S(1)} async-done(((bf16[16,48,512]{2,1,0:T(8,128)(2,1)}), bf16[16,48,512]{2,1,0:T(8,128)(2,1)S(1)}, u32[]{:S(2)}, u32[]{:S(2)}) %all-to-all-start) | async-done | bytes 786464 | tf_op jit(solution)/shard_map/all_to_all | solution.py:278
  56.2 0.1 shard_map.90
  56.3 0.2 collective-permute-done.5.came_high_ref
  56.5 0.0 collective-permute-done.3.came_feats_ref
  56.5 18.3 %all_to_all.20.tiles_ref = bf16[4,48,512]{2,1,0:T(8,128)(2,1)S(1)} all-to-all(bf16[4,48,512]{2,1,0:T(8,128)(2,1)S(1)} %shard_map.90), channel_id=1, replica_groups=mesh['yl'=2,'x'=4,'zh'=4,'zl'=4,'c'=2,'yh'=2] {'zh'}, dimensions={0} | all-to-all | bytes 393216 | tf_op jit(solution)/shard_map/all_to_all | solution.py:281
  74.8 0.7 shard_map.91
  75.5 7.5 %all-to-all-start.2 = ((bf16[4,48,512]{2,1,0:T(8,128)(2,1)}), bf16[4,48,512]{2,1,0:T(8,128)(2,1)S(1)}, u32[]{:S(2)}, u32[]{:S(2)}) async-start(bf16[4,48,512]{2,1,0:T(8,128)(2,1)} %shard_map.91), calls=%async_computation.2 | async-start | bytes 393216 | tf_op jit(solution)/shard_map/all_to_all | solution.py:290
  83.0 4.3 %shard_map.92 = (bf16[256,1024]{1,0:T(8,128)(2,1)}, bf16[256,768]{1,0:T(8,128)(2,1)}) custom-call(bf16[256,1024]{1,0:T(8,128)(2,1)} %bitcast.19, f32[256,1024]{1,0:T(8,128)} %get-tuple-element.73.grad_ref, bf16[256,256]{1,0:T(8,128)(2,1)} %get-tuple-element.74.weights_20_ref, bf16[256,1024]{1,0:T(8,128)(2,1)} %get-tuple-element.75.text_2_ref, ...), custom_call_target="tpu_custom_call" | custom-call | flops 536870912 | bytes 6160384 | tf_op jit(solution)/shard_map/pallas_call | solution.py:212
  87.3 0.8 all-to-all-done.2.tiles_ref
  88.1 0.1 shard_map.93
  88.2 15.5 %all_to_all.21 = bf16[16,48,512]{2,1,0:T(8,128)(2,1)S(1)} all-to-all(bf16[16,48,512]{2,1,0:T(8,128)(2,1)S(1)} %shard_map.93), channel_id=1, replica_groups=mesh['yl'=2,'x'=4,'zh'=4,'zl'=4,'c'=2,'yh'=2] {'yl','x','yh'}, dimensions={0} | all-to-all | bytes 1572864 | tf_op jit(solution)/shard_map/all_to_all | solution.py:293
  103.7 7.2 %collective-permute-start.6 = (bf16[768,512]{1,0:T(8,128)(2,1)S(1)}, bf16[768,512]{1,0:T(8,128)(2,1)S(1)}, u32[]{:S(2)}, u32[]{:S(2)}) collective-permute-start(bf16[768,512]{1,0:T(8,128)(2,1)S(1)} %bitcast.15), channel_id=1, source_target_pairs={{0,2},{2,0},{1,3},{3,1},{4,6},{6,4},{5,7},{7,5},{8,10},{10,8},{9,1... | collective-permute-start | bytes 2359304 | tf_op jit(solution)/shard_map/ppermute | solution.py:20
  110.9 1.9 %collective-permute-done.6.theirs_ref = bf16[768,512]{1,0:T(8,128)(2,1)S(1)} collective-permute-done((bf16[768,512]{1,0:T(8,128)(2,1)S(1)}, bf16[768,512]{1,0:T(8,128)(2,1)S(1)}, u32[]{:S(2)}, u32[]{:S(2)}) %collective-permute-start.6) | collective-permute-done | bytes 786464 | tf_op jit(solution)/shard_map/ppermute | solution.py:20
  112.8 1.3 %shard_map.94 = bf16[768,1024]{1,0:T(8,128)(2,1)} custom-call(s32[1]{0:T(128)} %bitcast.core_ref, bf16[768,512]{1,0:T(8,128)(2,1)S(1)} %bitcast.16, bf16[768,512]{1,0:T(8,128)(2,1)S(1)} %collective-permute-done.6.theirs_ref), custom_call_target="tpu_custom_call" | custom-call | bytes 3145728 | tf_op jit(solution)/shard_map/pallas_call | solution.py:212
  (12 shorter events, 0.0 us)
Async XLA Ops:
  0.6 16.2 %collective-permute-start = (bf16[256,1024]{1,0:T(8,128)(2,1)}, bf16[256,1024]{1,0:T(8,128)(2,1)S(1)}, u32[]{:S(2)}, u32[]{:S(2)}) collective-permute-start(bf16[256,1024]{1,0:T(8,128)(2,1)} %bitcast.17), channel_id=1, source_target_pairs={{0,510},{2,0},{4,2},{6,4},{8,6},{10,8},{12,10},{14,12},{16,14},{18... | collective-permute-start | bytes 1572872 | tf_op jit(solution)/shard_map/ppermute | solution.py:16
  9.4 14.3 %collective-permute-start.1 = (bf16[256,768]{1,0:T(8,128)(2,1)}, bf16[256,768]{1,0:T(8,128)(2,1)S(1)}, u32[]{:S(2)}, u32[]{:S(2)}) collective-permute-start(bf16[256,768]{1,0:T(8,128)(2,1)} %bitcast.21), channel_id=1, source_target_pairs={{0,4},{2,6},{4,8},{6,10},{8,12},{10,14},{12,16},{14,18},{16,20},{1... | collective-permute-start | bytes 1179656 | tf_op jit(solution)/shard_map/ppermute | solution.py:16
  16.9 6.9 %copy-start = (bf16[768,1024]{1,0:T(8,128)(2,1)S(1)}, bf16[768,1024]{1,0:T(8,128)(2,1)}, u32[]{:S(2)}) copy-start(bf16[768,1024]{1,0:T(8,128)(2,1)} %head_ref.7) | copy-start | bytes 4718596
  26.1 10.3 %collective-permute-start.2 = (bf16[768,512]{1,0:T(8,128)(2,1)S(1)}, bf16[768,512]{1,0:T(8,128)(2,1)S(1)}, u32[]{:S(2)}, u32[]{:S(2)}) collective-permute-start(bf16[768,512]{1,0:T(8,128)(2,1)S(1)} %get-tuple-element.58), channel_id=1, source_target_pairs={{0,2},{2,0},{1,3},{3,1},{4,6},{6,4},{5,7},{7,5},{8,10},{10,8},{9,1... | collective-permute-start | bytes 2359304 | tf_op jit(solution)/shard_map/ppermute | solution.py:20
  38.5 4.2 %copy-start.4 = (bf16[256,768]{1,0:T(8,128)(2,1)S(1)}, bf16[256,768]{1,0:T(8,128)(2,1)}, u32[]{:S(2)}) copy-start(bf16[256,768]{1,0:T(8,128)(2,1)} %get-tuple-element.66) | copy-start | bytes 1179652
  38.6 9.9 %copy-start.6 = (bf16[256,512]{1,0:T(8,128)(2,1)S(1)}, bf16[256,512]{1,0:T(8,128)(2,1)}, u32[]{:S(2)}) copy-start(bf16[256,512]{1,0:T(8,128)(2,1)} %get-tuple-element.68) | copy-start | bytes 786436
  38.6 11.8 %copy-start.5 = (bf16[256,512]{1,0:T(8,128)(2,1)S(1)}, bf16[256,512]{1,0:T(8,128)(2,1)}, u32[]{:S(2)}) copy-start(bf16[256,512]{1,0:T(8,128)(2,1)} %get-tuple-element.69) | copy-start | bytes 786436
  38.6 17.6 %all-to-all-start = ((bf16[16,48,512]{2,1,0:T(8,128)(2,1)}), bf16[16,48,512]{2,1,0:T(8,128)(2,1)S(1)}, u32[]{:S(2)}, u32[]{:S(2)}) async-start(bf16[16,48,512]{2,1,0:T(8,128)(2,1)} %shard_map.89), calls=%async_computation | async-start | bytes 1572864 | tf_op jit(solution)/shard_map/all_to_all | solution.py:278
  42.7 13.8 %collective-permute-start.3 = (bf16[256,768]{1,0:T(8,128)(2,1)S(1)}, bf16[256,768]{1,0:T(8,128)(2,1)S(1)}, u32[]{:S(2)}, u32[]{:S(2)}) collective-permute-start(bf16[256,768]{1,0:T(8,128)(2,1)S(1)} %copy-done.4), channel_id=1, source_target_pairs={{0,508},{2,510},{4,0},{6,2},{8,4},{10,6},{12,8},{14,10},{16,12},{1... | collective-permute-start | bytes 1179656 | tf_op jit(solution)/shard_map/ppermute | solution.py:16
  48.5 7.9 %collective-permute-start.4 = (bf16[256,512]{1,0:T(8,128)(2,1)S(1)}, bf16[256,512]{1,0:T(8,128)(2,1)S(1)}, u32[]{:S(2)}, u32[]{:S(2)}) collective-permute-start(bf16[256,512]{1,0:T(8,128)(2,1)S(1)} %copy-done.6), channel_id=1, source_target_pairs={{0,2},{2,4},{4,6},{6,8},{8,10},{10,12},{12,14},{14,16},{16,18},{18... | collective-permute-start | bytes 786440 | tf_op jit(solution)/shard_map/ppermute | solution.py:16
  50.4 6.1 %collective-permute-start.5 = (bf16[256,512]{1,0:T(8,128)(2,1)S(1)}, bf16[256,512]{1,0:T(8,128)(2,1)S(1)}, u32[]{:S(2)}, u32[]{:S(2)}) collective-permute-start(bf16[256,512]{1,0:T(8,128)(2,1)S(1)} %copy-done.5), channel_id=1, source_target_pairs={{0,2},{2,4},{4,6},{6,8},{8,10},{10,12},{12,14},{14,16},{16,18},{18... | collective-permute-start | bytes 786440 | tf_op jit(solution)/shard_map/ppermute | solution.py:16
  56.3 26.7 %copy-start.2 = (bf16[256,512]{1,0:T(8,128)(2,1)}, bf16[256,512]{1,0:T(8,128)(2,1)S(1)}, u32[]{:S(2)}) copy-start(bf16[256,512]{1,0:T(8,128)(2,1)S(1)} %collective-permute-done.4.came_low_ref) | copy-start | bytes 786436
  56.5 26.5 %copy-start.3 = (bf16[256,512]{1,0:T(8,128)(2,1)}, bf16[256,512]{1,0:T(8,128)(2,1)S(1)}, u32[]{:S(2)}) copy-start(bf16[256,512]{1,0:T(8,128)(2,1)S(1)} %collective-permute-done.5.came_high_ref) | copy-start | bytes 786436
  56.5 26.5 %copy-start.1 = (bf16[256,768]{1,0:T(8,128)(2,1)}, bf16[256,768]{1,0:T(8,128)(2,1)S(1)}, u32[]{:S(2)}) copy-start(bf16[256,768]{1,0:T(8,128)(2,1)S(1)} %collective-permute-done.3.came_feats_ref) | copy-start | bytes 1179652
  75.5 12.6 %all-to-all-start.2 = ((bf16[4,48,512]{2,1,0:T(8,128)(2,1)}), bf16[4,48,512]{2,1,0:T(8,128)(2,1)S(1)}, u32[]{:S(2)}, u32[]{:S(2)}) async-start(bf16[4,48,512]{2,1,0:T(8,128)(2,1)} %shard_map.91), calls=%async_computation.2 | async-start | bytes 393216 | tf_op jit(solution)/shard_map/all_to_all | solution.py:290
  103.7 9.1 %collective-permute-start.6 = (bf16[768,512]{1,0:T(8,128)(2,1)S(1)}, bf16[768,512]{1,0:T(8,128)(2,1)S(1)}, u32[]{:S(2)}, u32[]{:S(2)}) collective-permute-start(bf16[768,512]{1,0:T(8,128)(2,1)S(1)} %bitcast.15), channel_id=1, source_target_pairs={{0,2},{2,0},{1,3},{3,1},{4,6},{6,4},{5,7},{7,5},{8,10},{10,8},{9,1... | collective-permute-start | bytes 2359304 | tf_op jit(solution)/shard_map/ppermute | solution.py:20
